TPU v7x, 32 devices: a whole 2x2x4 slice. The times are simulated.
32 devices in a mesh: group: 2 (over x), blk: 16 (over z, y, core).
Axes of the slice: x: 2, y: 2, z: 4, core: 2. Of those that a mesh axis runs over, the one named last changes fastest.
Arguments:
- adjoint: float32 [10, 256, 8, 128], P('group', 'blk'), parts along dimension 0, may hold values from -6 to 6
- jac_diag: float32 [10, 5, 256, 8, 128], P('group', None, 'blk'), parts along dimension 0, may hold values from -2.5 to 2.5
- conv_mats: float32 [3, 5, 5], replicated, may hold values from -2.5 to 2.5
- face_scale: float32 [6, 256, 8, 128], P('group', 'blk'), parts along dimension 0, may hold values from 0.5 to 2
- kappa: float32 [512, 8, 128], P(('group', 'blk')), parts along dimension 0, may hold values from 0.1 to 1
- source: float32 [10, 256, 8, 128], P('group', 'blk'), parts along dimension 0, may hold values from -6 to 6
- box_of_row: int32 [65536, 1], P(('group', 'blk')), parts along dimension 0, may hold values from 0 to 15; in each aligned block of 2048 rows (0 to 2047, 2048 to 4095, ...) at most 256 rows name the same one
- lattice_cell: int32 [65536], P(('group', 'blk')), parts along dimension 0, may hold values from 0 to 3374
- lattice_frac: float32 [3, 65536], P(None, ('group', 'blk')), parts along dimension 1, may hold values from 0 to 1
- dres_dx: float32 [5, 3, 65536], P(None, None, ('group', 'blk')), parts along dimension 2, may hold values from -2.5 to 2.5
- dobj_dx: float32 [3, 65536], P(None, ('group', 'blk')), parts along dimension 1, may hold values from -6 to 6
Outputs:
- residual: float32 [10, 256, 8, 128], P('group', 'blk'), parts along dimension 0
- box_sens: float32 [6, 65536], P('group', 'blk'), parts along dimension 0
There are 2 independent parts, one for each index of `group`. A program takes and returns all parts, laid end to end along the dimension named above; an argument that names none is the same for every part. Nothing has to cross between parts.
Inputs may be any that keep to these rules, and one draw needn't show every extreme that they name: `box_of_row`: among the 2048 rows of one device no box is named more than 256 times, one box exactly 256 times in some devices' rows; every box is named somewhere.
All inputs are finite; a program needn't handle non-finite values.
Results may differ from a plain program's by a relative error of at most 0.0003.
Values sent between devices are 32-bit elements; how exact they have to be, the bound alone decides.
No kernel may reach another device: no remote copies, remote signals or barrier semaphores. Data moves between devices by JAX's collectives and lax.ppermute only.
A program may use at most 320 MiB of HBM per device.

v0:
```python
import functools

import jax
import jax.numpy as jnp
from jax import lax
from jax.experimental import pallas as pl
from jax.experimental.pallas import tpu as pltpu
from jax.sharding import PartitionSpec as P

LAT = 16
CHUNK = 256
SMALL = 12 * 2**20
F32 = jnp.float32
BF16 = jnp.bfloat16
NT = (((1,), (1,)), ((), ()))
NN = (((1,), (0,)), ((), ()))


def split_two(x):
    hi = x.astype(BF16)
    lo = (x - hi.astype(F32)).astype(BF16)
    return hi, lo


def on_even():
    return lax.axis_index("blk") % 2 == 0


def stay(*arrays):
    return [pltpu.with_memory_space_constraint(a, pltpu.HBM) for a in arrays]


def start_all(copies):
    for copy in copies:
        copy.start()
    return copies


def wait_all(copies):
    for copy in copies:
        copy.wait()


def pack_kernel(
    boxes,
    cap,
    adj_hbm,
    kap_hbm,
    box_hbm,
    cell_hbm,
    frac_hbm,
    dres_hbm,
    dobj_hbm,
    out_ref,
    mate_ref,
    other_ref,
    adj_ref,
    kap_ref,
    box_ref,
    cell_ref,
    frac_ref,
    dres_ref,
    dobj_ref,
    ranks_ref,
    sems,
):
    fields, planes, _, lanes = adj_hbm.shape
    rows = planes * lanes
    ends = (0, planes - 1)
    moves = [(box_hbm, box_ref), (dres_hbm, dres_ref), (adj_hbm, adj_ref)]
    moves += [(dobj_hbm, dobj_ref), (frac_hbm, frac_ref), (cell_hbm, cell_ref)]
    moves += [(kap_hbm.at[x], kap_ref.at[i]) for i, x in enumerate(ends)]
    copies = start_all(
        [pltpu.make_async_copy(src, dst, sems.at[i]) for i, (src, dst) in enumerate(moves)]
    )
    copies[0].wait()
    box = box_ref[...]

    chunks = rows // CHUNK
    names = lax.broadcasted_iota(jnp.int32, (boxes, CHUNK), 0)
    hot = [(box[:, j * CHUNK:(j + 1) * CHUNK] == names).astype(F32) for j in range(chunks)]
    earlier = (
        lax.broadcasted_iota(jnp.int32, (CHUNK, CHUNK), 0)
        < lax.broadcasted_iota(jnp.int32, (CHUNK, CHUNK), 1)
    ).astype(F32).astype(BF16)
    counts = lax.dot_general(
        jnp.concatenate(hot, 0).astype(BF16), earlier, NN, preferred_element_type=F32
    )
    offset = jnp.zeros((boxes, 1), F32)
    for j in range(chunks):
        here = counts[j * boxes:(j + 1) * boxes]
        ranks_ref[:, j * CHUNK:(j + 1) * CHUNK] = jnp.sum(
            hot[j] * (here + offset), axis=0, keepdims=True
        )
        offset = offset + here[:, CHUNK - 1:] + hot[j][:, CHUNK - 1:]

    wait_all(copies[1:])
    even = on_even()
    for f in range(fields + 1):
        first = adj_ref[f, 0] if f < fields else kap_ref[0]
        last = adj_ref[f, planes - 1] if f < fields else kap_ref[1]
        mate_ref[f] = jnp.where(even, last, first)
        other_ref[f] = jnp.where(even, first, last)

    total = jnp.zeros((boxes * 16, cap), F32)
    slots = lax.broadcasted_iota(jnp.int32, (cap, CHUNK), 0).astype(F32)
    per = CHUNK // lanes
    for j in range(chunks):
        part = slice(j * CHUNK, (j + 1) * CHUNK)
        acc = dobj_ref[:, part]
        for k in range(fields):
            psi = jnp.concatenate(
                [adj_ref[k, x, 0:1, :] for x in range(j * per, (j + 1) * per)], 1
            )
            acc = acc - dres_ref[k, :, part] * psi
        values = jnp.concatenate(
            [acc, frac_ref[:, part], cell_ref[:, part].astype(F32), jnp.zeros((1, CHUNK), F32)], 0
        )
        hi = values.astype(BF16).astype(F32)
        both = jnp.concatenate([hi, values - hi], 0)
        mine = box[:, part]
        lhs = jnp.concatenate(
            [jnp.where(mine == b, both, 0.0) for b in range(boxes)], 0
        ).astype(BF16)
        rhs = (slots == ranks_ref[:, part]).astype(F32).astype(BF16)
        total = total + lax.dot_general(lhs, rhs, NT, preferred_element_type=F32)
    for b in range(boxes):
        out_ref[b] = total[b * 16:b * 16 + 8] + total[b * 16 + 8:b * 16 + 16]


def plane_residual(psi, kap, below, above, jac, face, src, conv):
    fields = len(psi)
    rows, lanes = kap.shape
    row = lax.broadcasted_iota(jnp.int32, (rows, lanes), 0)
    lane = lax.broadcasted_iota(jnp.int32, (rows, lanes), 1)
    masks = ((row < rows - 1, row > 0), (lane < lanes - 1, lane > 0))

    def sides(value, dim):
        size = value.shape[dim]
        up = jnp.where(masks[dim][0], pltpu.roll(value, size - 1, dim), 0.0)
        down = jnp.where(masks[dim][1], pltpu.roll(value, 1, dim), 0.0)
        return up, down

    centre = list(psi) + [kap]
    result = []
    for f in range(fields):
        total = jac(0, f) * psi[0]
        for k in range(1, fields):
            total = total + jac(k, f) * psi[k]
        result.append(total - src(f))
    spread = None
    for d in range(3):
        pair = list(zip(above, below)) if d == 0 else [sides(v, d - 1) for v in centre]
        scale = 0.5 * face(d)
        diff = [scale * (pair[k][0] - pair[k][1]) for k in range(fields)]
        up = 0.5 * (kap + pair[fields][0])
        down = 0.5 * (kap + pair[fields][1])
        spread = up + down if spread is None else spread + up + down
        for f in range(fields):
            total = result[f]
            for k in range(fields):
                total = total + conv[k, d, f] * diff[k]
            result[f] = total - up * pair[f][0] - down * pair[f][1]
    return [result[f] + spread * psi[f] for f in range(fields)]


def inner_kernel(
    adj_hbm,
    jac_hbm,
    conv_hbm,
    face_hbm,
    kap_hbm,
    src_hbm,
    after_hbm,
    out_hbm,
    adj_ref,
    jac_ref,
    conv_ref,
    face_ref,
    kap_ref,
    src_ref,
    out_ref,
    sems,
    out_sems,
):
    fields, planes, _, _ = adj_hbm.shape
    steps = 4
    cuts = [1 + (planes - 2) * i // steps for i in range(steps + 1)]
    pieces = [slice(a, b) for a, b in zip(cuts[:-1], cuts[1:])]
    moves = [(adj_hbm, adj_ref), (kap_hbm, kap_ref), (conv_hbm, conv_ref)]
    for p in pieces:
        moves.append((jac_hbm.at[:, :, p], jac_ref.at[:, :, p]))
        moves.append((src_hbm.at[:, p], src_ref.at[:, p]))
        moves.append((face_hbm.at[:, p], face_ref.at[:, p]))
    copies = start_all(
        [pltpu.make_async_copy(src, dst, sems.at[i]) for i, (src, dst) in enumerate(moves)]
    )
    wait_all(copies[:3])
    sent = []
    for i, p in enumerate(pieces):
        wait_all(copies[3 + 3 * i:6 + 3 * i])
        for x in range(p.start, p.stop):
            def at(y):
                return [adj_ref[f, y] for f in range(fields)] + [kap_ref[y]]

            here = at(x)
            planes_of = plane_residual(
                here[:fields],
                here[fields],
                at(x - 1),
                at(x + 1),
                lambda k, f: jac_ref[k, f, x],
                lambda d: face_ref[d, x],
                lambda f: src_ref[f, x],
                conv_ref,
            )
            for f in range(fields):
                out_ref[f, x] = planes_of[f]
        copy = pltpu.make_async_copy(out_ref.at[:, p], out_hbm.at[:, p], out_sems.at[i])
        copy.start()
        sent.append(copy)
    wait_all(sent)


def sum_kernel(
    got_ref,
    adj_hbm,
    jac_hbm,
    conv_hbm,
    face_hbm,
    kap_hbm,
    src_hbm,
    mate_ref,
    other_ref,
    part_hbm,
    out_ref,
    res_hbm,
    adj_ref,
    jac_ref,
    conv_ref,
    face_ref,
    kap_ref,
    src_ref,
    res_ref,
    sems,
    out_sems,
):
    del part_hbm
    fields, planes, _, _ = adj_hbm.shape
    ends = (0, planes - 1)
    moves = [(conv_hbm, conv_ref)]
    for i, x in enumerate(ends):
        near = pl.ds(0 if i == 0 else planes - 2, 2)
        moves.append((adj_hbm.at[:, near], adj_ref.at[i]))
        moves.append((kap_hbm.at[near], kap_ref.at[i]))
        moves.append((jac_hbm.at[:, :, x], jac_ref.at[i]))
        moves.append((src_hbm.at[:, x], src_ref.at[i]))
        moves.append((face_hbm.at[:, x], face_ref.at[i]))
    copies = start_all(
        [pltpu.make_async_copy(src, dst, sems.at[i]) for i, (src, dst) in enumerate(moves)]
    )

    sources, _, cap = got_ref.shape
    inner = LAT - 1
    points = lax.broadcasted_iota(jnp.int32, (LAT, cap), 0).astype(F32)
    both = jnp.zeros((6 * LAT, LAT * LAT), F32)
    for s in range(sources):
        block = got_ref[s]
        cell = block[6:7]
        first = jnp.floor((cell + 0.5) * (1.0 / (inner * inner)))
        rest = cell - first * (inner * inner)
        second = jnp.floor((rest + 0.5) * (1.0 / inner))
        third = rest - second * inner
        tent = []
        for d, low in enumerate((first, second, third)):
            u = block[3 + d:4 + d]
            tent.append(
                jnp.where(points == low, 1.0 - u, 0.0) + jnp.where(points == low + 1.0, u, 0.0)
            )
        left = jnp.concatenate([tent[0] * block[c:c + 1] for c in range(3)], 0)
        right = jnp.concatenate([tent[1][b:b + 1] * tent[2] for b in range(LAT)], 0)
        left_hi, left_lo = split_two(left)
        right_hi, right_lo = split_two(right)
        lhs = jnp.concatenate([left_hi, left_lo], 0)
        both = both + lax.dot_general(lhs, right_hi, NT, preferred_element_type=F32)
        both = both + lax.dot_general(lhs, right_lo, NT, preferred_element_type=F32)

    wait_all(copies)
    even = on_even()
    sent = []
    for i, x in enumerate(ends):
        pair = [[adj_ref[i, f, j] for f in range(fields)] + [kap_ref[i, j]] for j in (0, 1)]
        beyond = [
            jnp.where(even == (i == 0), other_ref[f], mate_ref[f]) for f in range(fields + 1)
        ]
        here = pair[i]
        planes_of = plane_residual(
            here[:fields],
            here[fields],
            beyond if i == 0 else pair[0],
            pair[1] if i == 0 else beyond,
            lambda k, f: jac_ref[i, k, f],
            lambda d: face_ref[i, d],
            lambda f: src_ref[i, f],
            conv_ref,
        )
        for f in range(fields):
            res_ref[i, f] = planes_of[f]
        copy = pltpu.make_async_copy(res_ref.at[i], res_hbm.at[:, x], out_sems.at[i])
        copy.start()
        sent.append(copy)
    result = both[:3 * LAT] + both[3 * LAT:]
    for c in range(3):
        for a in range(LAT):
            out_ref[c:c + 1, a * LAT * LAT:(a + 1) * LAT * LAT] = result[c * LAT + a:c * LAT + a + 1]
    wait_all(sent)


def local(
    adjoint,
    jac_diag,
    conv_mats,
    face_scale,
    kappa,
    source,
    box_of_row,
    lattice_cell,
    lattice_frac,
    dres_dx,
    dobj_dx,
):
    boxes = lax.axis_size("blk")
    rows = box_of_row.shape[0]
    cap = 2 * rows // boxes
    fields, planes = adjoint.shape[:2]
    plane = adjoint.shape[2:]
    vmem = pl.BlockSpec(memory_space=pltpu.VMEM)
    hbm = pl.BlockSpec(memory_space=pltpu.HBM)
    params = pltpu.CompilerParams(vmem_limit_bytes=SMALL)
    conv = conv_mats.transpose(1, 0, 2)
    box_row = box_of_row.reshape(1, rows)
    cell_row = lattice_cell.reshape(1, rows)
    box_row, cell_row, conv, adjoint, jac_diag, face_scale, kappa, source = stay(
        box_row, cell_row, conv, adjoint, jac_diag, face_scale, kappa, source
    )
    lattice_frac, dres_dx, dobj_dx = stay(lattice_frac, dres_dx, dobj_dx)

    def shape(*dims):
        return jax.ShapeDtypeStruct(dims, F32)

    packed, to_mate, to_other = pl.pallas_call(
        functools.partial(pack_kernel, boxes, cap),
        out_shape=(shape(boxes, 8, cap), shape(fields + 1, *plane), shape(fields + 1, *plane)),
        in_specs=[hbm] * 7,
        out_specs=(vmem, vmem, vmem),
        scratch_shapes=[
            pltpu.VMEM(adjoint.shape, F32),
            pltpu.VMEM((2,) + plane, F32),
            pltpu.VMEM((1, rows), jnp.int32),
            pltpu.VMEM((1, rows), jnp.int32),
            pltpu.VMEM(lattice_frac.shape, F32),
            pltpu.VMEM(dres_dx.shape, F32),
            pltpu.VMEM(dobj_dx.shape, F32),
            pltpu.VMEM((1, rows), F32),
            pltpu.SemaphoreType.DMA((8,)),
        ],
        compiler_params=params,
        name="pack_rows",
    )(adjoint, kappa, box_row, cell_row, lattice_frac, dres_dx, dobj_dx)
    got = lax.all_to_all(packed, "blk", 0, 0, tiled=True)

    pairs = [(i, i + 1) for i in range(boxes - 1)]
    both_ways = [[p for i, j in pairs if i % 2 == turn for p in ((i, j), (j, i))] for turn in (0, 1)]
    mate = lax.ppermute(to_mate, "blk", both_ways[0])
    other = lax.ppermute(to_other, "blk", both_ways[1])

    inner = pl.pallas_call(
        inner_kernel,
        out_shape=shape(*adjoint.shape),
        in_specs=[hbm] * 6 + [pl.BlockSpec(memory_space=pl.ANY)],
        out_specs=hbm,
        scratch_shapes=[
            pltpu.VMEM(adjoint.shape, F32),
            pltpu.VMEM(jac_diag.shape, F32),
            pltpu.SMEM(conv.shape, F32),
            pltpu.VMEM(face_scale.shape, F32),
            pltpu.VMEM(kappa.shape, F32),
            pltpu.VMEM(source.shape, F32),
            pltpu.VMEM(adjoint.shape, F32),
            pltpu.SemaphoreType.DMA((15,)),
            pltpu.SemaphoreType.DMA((4,)),
        ],
        compiler_params=params,
        name="sweep_inner",
    )(adjoint, jac_diag, conv, face_scale, kappa, source, to_mate)

    box_sens, residual = pl.pallas_call(
        sum_kernel,
        out_shape=(shape(3, LAT**3), shape(*adjoint.shape)),
        in_specs=[vmem] + [hbm] * 6 + [vmem, vmem, hbm],
        out_specs=(vmem, hbm),
        scratch_shapes=[
            pltpu.VMEM((2, fields, 2) + plane, F32),
            pltpu.VMEM((2, fields, fields) + plane, F32),
            pltpu.SMEM(conv.shape, F32),
            pltpu.VMEM((2, 3) + plane, F32),
            pltpu.VMEM((2, 2) + plane, F32),
            pltpu.VMEM((2, fields) + plane, F32),
            pltpu.VMEM((2, fields) + plane, F32),
            pltpu.SemaphoreType.DMA((11,)),
            pltpu.SemaphoreType.DMA((2,)),
        ],
        input_output_aliases={9: 1},
        compiler_params=params,
        name="sum_rows",
    )(got, adjoint, jac_diag, conv, face_scale, kappa, source, mate, other, inner)
    return residual, box_sens


def solution(mesh):
    in_specs = (
        P("group", "blk", None, None),
        P("group", None, "blk", None, None),
        P(),
        P("group", "blk", None, None),
        P(("group", "blk"), None, None),
        P("group", "blk", None, None),
        P(("group", "blk"), None),
        P(("group", "blk")),
        P(None, ("group", "blk")),
        P(None, None, ("group", "blk")),
        P(None, ("group", "blk")),
    )
    out_specs = (P("group", "blk", None, None), P("group", "blk"))
    return jax.shard_map(local, mesh=mesh, in_specs=in_specs, out_specs=out_specs, check_vma=False)
```

profile of v0, /device:TPU:0, one launch (start us, length us, event | category | flops | bytes accessed | tf_op | source)
XLA Modules:
  0.0 22.1 jit_solution(13816333321839652827)
XLA Ops:
  0.6 2.3 %pack_rows.1 = (f32[16,8,256]{2,1,0:T(8,128)}, f32[6,8,128]{2,1,0:T(8,128)S(1)}, f32[6,8,128]{2,1,0:T(8,128)S(1)}) custom-call(f32[5,16,8,128]{3,2,1,0:T(8,128)} %adj_hbm.5, f32[16,8,128]{2,1,0:T(8,128)} %kap_hbm.5, s32[1,2048]{1,0:T(1,128)} %bitcast.5, s32[1,2048]{1,0:T(1,128)} %bitcast.6, f32[3,2048]{1,0:T(4,128)} %frac_hbm.1, f32[5,3,2048]{2,1,0:T(4,128)} %dres_hbm.1, ...), custom_call_target="tpu_custom_call" | custom-call | tf_op jit(solution)/shard_map/pack_rows/pallas_call | solution.py:351
  3.0 7.4 %all-to-all-start = ((f32[16,8,256]{2,1,0:T(8,128)}), f32[16,8,256]{2,1,0:T(8,128)S(1)}, u32[]{:S(2)}, u32[]{:S(2)}) async-start(f32[16,8,256]{2,1,0:T(8,128)} %get-tuple-element.7), calls=%async_computation | async-start | bytes 262144 | tf_op jit(solution)/shard_map/all_to_all | solution.py:370
  10.4 0.7 %collective-permute-start.1 = (f32[6,8,128]{2,1,0:T(8,128)S(1)}, f32[6,8,128]{2,1,0:T(8,128)S(1)}, u32[]{:S(2)}, u32[]{:S(2)}) collective-permute-start(f32[6,8,128]{2,1,0:T(8,128)S(1)} %get-tuple-element.9), channel_id=1, source_target_pairs={{1,2},{2,1},{3,4},{4,3},{5,6},{6,5},{7,8},{8,7},{9,10},{10,9},{11,... | collective-permute-start | bytes 73736 | tf_op jit(solution)/shard_map/ppermute | solution.py:375
  11.0 3.3 %collective-permute-start = (f32[6,8,128]{2,1,0:T(8,128)S(1)}, f32[6,8,128]{2,1,0:T(8,128)S(1)}, u32[]{:S(2)}, u32[]{:S(2)}) collective-permute-start(f32[6,8,128]{2,1,0:T(8,128)S(1)} %get-tuple-element.8.after_hbm), channel_id=1, source_target_pairs={{0,1},{1,0},{2,3},{3,2},{4,5},{5,4},{6,7},{7,6},{8,9},{9,8},{10,11... | collective-permute-start | bytes 73736 | tf_op jit(solution)/shard_map/ppermute | solution.py:374
  14.4 2.8 %sweep_inner.1.part_hbm = f32[5,16,8,128]{3,2,1,0:T(8,128)} custom-call(f32[5,16,8,128]{3,2,1,0:T(8,128)} %adj_hbm.5, f32[5,5,16,8,128]{4,3,2,1,0:T(8,128)} %jac_hbm.3, f32[5,3,5]{2,1,0:T(4,128)} %bitcast.3, f32[3,16,8,128]{3,2,1,0:T(8,128)} %face_hbm.3, f32[16,8,128]{2,1,0:T(8,128)} %kap_hbm.5, f32[5,16,8,128]{3,2,1,0:T(8,128)} %src_hbm.3, ...), custom_call_target="tpu_custom_call" | custom-call | tf_op jit(solution)/shard_map/sweep_inner/pallas_call | solution.py:377
  17.2 0.0 collective-permute-done.1.other_ref
  17.2 0.0 collective-permute-done.mate_ref
  17.2 1.1 %all-to-all-done.got_ref = f32[16,8,256]{2,1,0:T(8,128)S(1)} async-done(((f32[16,8,256]{2,1,0:T(8,128)}), f32[16,8,256]{2,1,0:T(8,128)S(1)}, u32[]{:S(2)}, u32[]{:S(2)}) %all-to-all-start) | async-done | bytes 131104 | tf_op jit(solution)/shard_map/all_to_all | solution.py:370
  18.3 3.8 %sum_rows.1 = (f32[3,4096]{1,0:T(4,128)}, f32[5,16,8,128]{3,2,1,0:T(8,128)}) custom-call(f32[16,8,256]{2,1,0:T(8,128)S(1)} %all-to-all-done.got_ref, f32[5,16,8,128]{3,2,1,0:T(8,128)} %adj_hbm.5, f32[5,5,16,8,128]{4,3,2,1,0:T(8,128)} %jac_hbm.3, f32[5,3,5]{2,1,0:T(4,128)} %bitcast.4, f32[3,16,8,128]{3,2,1,0:T(8,128)} %face_hbm.3, ...), custom_call_target="tpu_custom_call", output_to_operand_aliasing={{1}: (9, {})} | custom-call | tf_op jit(solution)/shard_map/sum_rows/pallas_call | solution.py:397
Async XLA Ops:
  3.0 15.3 %all-to-all-start = ((f32[16,8,256]{2,1,0:T(8,128)}), f32[16,8,256]{2,1,0:T(8,128)S(1)}, u32[]{:S(2)}, u32[]{:S(2)}) async-start(f32[16,8,256]{2,1,0:T(8,128)} %get-tuple-element.7), calls=%async_computation | async-start | bytes 262144 | tf_op jit(solution)/shard_map/all_to_all | solution.py:370
  10.4 6.8 %collective-permute-start.1 = (f32[6,8,128]{2,1,0:T(8,128)S(1)}, f32[6,8,128]{2,1,0:T(8,128)S(1)}, u32[]{:S(2)}, u32[]{:S(2)}) collective-permute-start(f32[6,8,128]{2,1,0:T(8,128)S(1)} %get-tuple-element.9), channel_id=1, source_target_pairs={{1,2},{2,1},{3,4},{4,3},{5,6},{6,5},{7,8},{8,7},{9,10},{10,9},{11,... | collective-permute-start | bytes 73736 | tf_op jit(solution)/shard_map/ppermute | solution.py:375
  11.0 6.2 %collective-permute-start = (f32[6,8,128]{2,1,0:T(8,128)S(1)}, f32[6,8,128]{2,1,0:T(8,128)S(1)}, u32[]{:S(2)}, u32[]{:S(2)}) collective-permute-start(f32[6,8,128]{2,1,0:T(8,128)S(1)} %get-tuple-element.8.after_hbm), channel_id=1, source_target_pairs={{0,1},{1,0},{2,3},{3,2},{4,5},{5,4},{6,7},{7,6},{8,9},{9,8},{10,11... | collective-permute-start | bytes 73736 | tf_op jit(solution)/shard_map/ppermute | solution.py:374
where the time goes:
time: 22.4 us; the launch traced here: 22.1 us
  starting transfers between devices  11.4 us (51%)
  Pallas kernels  8.93 us (40%)
  waiting for transfers between devices  1.08 us (5%)
  between operations  0.68 us (3%)
    all_to_all x1, starting transfers between devices, local(): got = lax.all_to_all(packed, 'blk', 0, 0, tiled=True)  7.4 us
    pallas_call x1, Pallas kernels, local(): pl.pallas_call(sum_kernel, out_shape=(shape(3, LAT ** 3), shape(*adjoint....  3.77 us
    ppermute x1, starting transfers between devices, local(): mate = lax.ppermute(to_mate, 'blk', both_ways[0])  3.34 us
    pallas_call x1, Pallas kernels, local(): pl.pallas_call(inner_kernel, out_shape=shape(*adjoint.shape), in_specs=[h...  2.82 us
    pallas_call x1, Pallas kernels, local(): pl.pallas_call(functools.partial(pack_kernel, boxes, cap), out_shape=(sha...  2.33 us
    all_to_all x1, waiting for transfers between devices, local(): got = lax.all_to_all(packed, 'blk', 0, 0, tiled=True)  1.07 us
    ppermute x1, starting transfers between devices, local(): other = lax.ppermute(to_other, 'blk', both_ways[1])  0.66 us
  transfers between devices with their start and end apart: 3, of which 1 were waited for; matrix products, arithmetic and copies ran while one was open for 0% of the time, Pallas kernels for 13%

commit v1 on v0

--- a/solution.py
+++ b/solution.py
@@ -51,7 +51,8 @@
     frac_hbm,
     dres_hbm,
     dobj_hbm,
-    out_ref,
+    own_ref,
+    give_ref,
     mate_ref,
     other_ref,
     adj_ref,
@@ -96,6 +97,8 @@
 
     wait_all(copies[1:])
     even = on_even()
+    core = lax.axis_index("blk") % 2
+    order = [2 * j + core for j in range(boxes // 2)] + [2 * j + 1 - core for j in range(boxes // 2)]
     for f in range(fields + 1):
         first = adj_ref[f, 0] if f < fields else kap_ref[0]
         last = adj_ref[f, planes - 1] if f < fields else kap_ref[1]
@@ -120,12 +123,19 @@
         both = jnp.concatenate([hi, values - hi], 0)
         mine = box[:, part]
         lhs = jnp.concatenate(
-            [jnp.where(mine == b, both, 0.0) for b in range(boxes)], 0
+            [jnp.where(mine == b, both, 0.0) for b in order], 0
         ).astype(BF16)
         rhs = (slots == ranks_ref[:, part]).astype(F32).astype(BF16)
         total = total + lax.dot_general(lhs, rhs, NT, preferred_element_type=F32)
     for b in range(boxes):
-        out_ref[b] = total[b * 16:b * 16 + 8] + total[b * 16 + 8:b * 16 + 16]
+        target = own_ref if b < boxes // 2 else give_ref
+        target[b % (boxes // 2)] = total[b * 16:b * 16 + 8] + total[b * 16 + 8:b * 16 + 16]
+
+
+def merge_kernel(own_ref, got_ref, out_ref):
+    for j in range(own_ref.shape[0]):
+        out_ref[j, 0] = own_ref[j]
+        out_ref[j, 1] = got_ref[j]
 
 
 def plane_residual(psi, kap, below, above, jac, face, src, conv):
@@ -348,11 +358,17 @@
     def shape(*dims):
         return jax.ShapeDtypeStruct(dims, F32)
 
-    packed, to_mate, to_other = pl.pallas_call(
+    half = boxes // 2
+    own, give, to_mate, to_other = pl.pallas_call(
         functools.partial(pack_kernel, boxes, cap),
-        out_shape=(shape(boxes, 8, cap), shape(fields + 1, *plane), shape(fields + 1, *plane)),
+        out_shape=(
+            shape(half, 8, cap),
+            shape(half, 8, cap),
+            shape(fields + 1, *plane),
+            shape(fields + 1, *plane),
+        ),
         in_specs=[hbm] * 7,
-        out_specs=(vmem, vmem, vmem),
+        out_specs=(vmem,) * 4,
         scratch_shapes=[
             pltpu.VMEM(adjoint.shape, F32),
             pltpu.VMEM((2,) + plane, F32),
@@ -367,12 +383,23 @@
         compiler_params=params,
         name="pack_rows",
     )(adjoint, kappa, box_row, cell_row, lattice_frac, dres_dx, dobj_dx)
-    got = lax.all_to_all(packed, "blk", 0, 0, tiled=True)
-
     pairs = [(i, i + 1) for i in range(boxes - 1)]
     both_ways = [[p for i, j in pairs if i % 2 == turn for p in ((i, j), (j, i))] for turn in (0, 1)]
+    taken = lax.ppermute(give, "blk", both_ways[0])
     mate = lax.ppermute(to_mate, "blk", both_ways[0])
     other = lax.ppermute(to_other, "blk", both_ways[1])
+
+    merged = pl.pallas_call(
+        merge_kernel,
+        out_shape=shape(half, 2, 8, cap),
+        in_specs=[vmem, vmem],
+        out_specs=vmem,
+        compiler_params=params,
+        name="merge_rows",
+    )(own, taken)
+    same_core = [list(range(c, boxes, 2)) for c in (0, 1)]
+    got = lax.all_to_all(merged, "blk", 0, 0, axis_index_groups=same_core, tiled=True)
+    got = got.reshape(boxes, 8, cap)
 
     inner = pl.pallas_call(
         inner_kernel,
@@ -392,7 +419,7 @@
         ],
         compiler_params=params,
         name="sweep_inner",
-    )(adjoint, jac_diag, conv, face_scale, kappa, source, to_mate)
+    )(adjoint, jac_diag, conv, face_scale, kappa, source, merged)
 
     box_sens, residual = pl.pallas_call(
         sum_kernel,

time: 22.4 us -> 23 us (1.027)
  waiting for transfers between devices: 1.08 us -> 4.72 us
  starting transfers between devices: 11.4 us -> 8.36 us
    ppermute x1, starting transfers between devices: 3.34 us -> 0.01 us  [local(): mate = lax.ppermute(to_mate, 'blk', both_ways[0])]
    all_to_all x1, waiting for transfers between devices: 1.07 us -> 3.81 us  [local(): lax.all_to_all(merged, 'blk', 0, 0, axis_index_groups=same_core, tiled=True)]
    ppermute x0 -> x1, waiting for transfers between devices: none -> 0.9 us  [local(): taken = lax.ppermute(give, 'blk', both_ways[0])]
    pallas_call x0 -> x1, Pallas kernels: none -> 0.66 us  [local(): pl.pallas_call(merge_kernel, out_shape=shape(half, 2, 8, cap), in_specs=[...]
    pallas_call x1, Pallas kernels: 2.33 us -> 1.7 us  [local(): pl.pallas_call(functools.partial(pack_kernel, boxes, cap), out_shape=(sha...]
    ppermute x0 -> x1, starting transfers between devices: none -> 0.52 us  [local(): taken = lax.ppermute(give, 'blk', both_ways[0])]
  transfers between devices with their start and end apart: 3 -> 4, of which waited for: 1 -> 2; matrix products, arithmetic and copies ran while one was open for 0% -> 0% of each run, Pallas kernels for 13% -> 12%
where the time goes in v1:
time: 23 us; the launch traced here: 22.7 us
  Pallas kernels  8.95 us (39%)
  starting transfers between devices  8.36 us (36%)
  waiting for transfers between devices  4.72 us (21%)
  between operations  0.68 us (3%)
    all_to_all x1, starting transfers between devices, local(): lax.all_to_all(merged, 'blk', 0, 0, axis_index_groups=same_core, tiled=True)  7.18 us
    all_to_all x1, waiting for transfers between devices, local(): lax.all_to_all(merged, 'blk', 0, 0, axis_index_groups=same_core, tiled=True)  3.81 us
    pallas_call x1, Pallas kernels, local(): pl.pallas_call(sum_kernel, out_shape=(shape(3, LAT ** 3), shape(*adjoint....  3.77 us
    pallas_call x1, Pallas kernels, local(): pl.pallas_call(inner_kernel, out_shape=shape(*adjoint.shape), in_specs=[h...  2.83 us
    pallas_call x1, Pallas kernels, local(): pl.pallas_call(functools.partial(pack_kernel, boxes, cap), out_shape=(sha...  1.7 us
    ppermute x1, waiting for transfers between devices, local(): taken = lax.ppermute(give, 'blk', both_ways[0])  0.9 us
    ppermute x1, starting transfers between devices, local(): other = lax.ppermute(to_other, 'blk', both_ways[1])  0.66 us
    pallas_call x1, Pallas kernels, local(): pl.pallas_call(merge_kernel, out_shape=shape(half, 2, 8, cap), in_specs=[...  0.66 us
  transfers between devices with their start and end apart: 4, of which 2 were waited for; matrix products, arithmetic and copies ran while one was open for 0% of the time, Pallas kernels for 12%

profile of v1, /device:TPU:0, one launch (start us, length us, event | category | flops | bytes accessed | tf_op | source)
XLA Modules:
  0.0 22.7 jit_solution(17933279139596204202)
XLA Ops:
  0.6 1.7 %pack_rows.1 = (f32[8,8,256]{2,1,0:T(8,128)S(1)}, f32[8,8,256]{2,1,0:T(8,128)S(1)}, f32[6,8,128]{2,1,0:T(8,128)S(1)}, f32[6,8,128]{2,1,0:T(8,128)S(1)}) custom-call(f32[5,16,8,128]{3,2,1,0:T(8,128)} %adj_hbm.5, f32[16,8,128]{2,1,0:T(8,128)} %kap_hbm.5, s32[1,2048]{1,0:T(1,128)} %bitcast.7, s32[1,2048]{1,0:T(1,128)} %bitcast.8, f32[3,2048]{1,0:T(4,128)} %frac_hbm.1, ...), custom_call_target="tpu_custom_call" | custom-call | tf_op jit(solution)/shard_map/pack_rows/pallas_call | solution.py:362
  2.3 0.5 %collective-permute-start = (f32[8,8,256]{2,1,0:T(8,128)S(1)}, f32[8,8,256]{2,1,0:T(8,128)S(1)}, u32[]{:S(2)}, u32[]{:S(2)}) collective-permute-start(f32[8,8,256]{2,1,0:T(8,128)S(1)} %get-tuple-element.9), channel_id=1, source_target_pairs={{0,1},{1,0},{2,3},{3,2},{4,5},{5,4},{6,7},{7,6},{8,9},{9,8},{10,11... | collective-permute-start | bytes 196616 | tf_op jit(solution)/shard_map/ppermute | solution.py:388
  2.9 0.9 %collective-permute-done.got_ref = f32[8,8,256]{2,1,0:T(8,128)S(1)} collective-permute-done((f32[8,8,256]{2,1,0:T(8,128)S(1)}, f32[8,8,256]{2,1,0:T(8,128)S(1)}, u32[]{:S(2)}, u32[]{:S(2)}) %collective-permute-start) | collective-permute-done | bytes 65568 | tf_op jit(solution)/shard_map/ppermute | solution.py:388
  3.8 0.7 %merge_rows.1.after_hbm = f32[8,2,8,256]{3,2,1,0:T(8,128)} custom-call(f32[8,8,256]{2,1,0:T(8,128)S(1)} %get-tuple-element.8.own_ref, f32[8,8,256]{2,1,0:T(8,128)S(1)} %collective-permute-done.got_ref), custom_call_target="tpu_custom_call" | custom-call | tf_op jit(solution)/shard_map/merge_rows/pallas_call | solution.py:392
  4.4 7.2 %all-to-all-start = ((f32[8,2,8,256]{3,2,1,0:T(8,128)}), f32[8,2,8,256]{3,2,1,0:T(8,128)S(1)}, u32[]{:S(2)}, u32[]{:S(2)}) async-start(f32[8,2,8,256]{3,2,1,0:T(8,128)} %merge_rows.1.after_hbm), calls=%async_computation | async-start | bytes 262144 | tf_op jit(solution)/shard_map/all_to_all | solution.py:401
  11.6 0.0 collective-permute-start.1
  11.6 0.7 %collective-permute-start.2 = (f32[6,8,128]{2,1,0:T(8,128)S(1)}, f32[6,8,128]{2,1,0:T(8,128)S(1)}, u32[]{:S(2)}, u32[]{:S(2)}) collective-permute-start(f32[6,8,128]{2,1,0:T(8,128)S(1)} %get-tuple-element.11), channel_id=1, source_target_pairs={{1,2},{2,1},{3,4},{4,3},{5,6},{6,5},{7,8},{8,7},{9,10},{10,9},{11,... | collective-permute-start | bytes 73736 | tf_op jit(solution)/shard_map/ppermute | solution.py:390
  12.3 2.8 %sweep_inner.1.part_hbm = f32[5,16,8,128]{3,2,1,0:T(8,128)} custom-call(f32[5,16,8,128]{3,2,1,0:T(8,128)} %adj_hbm.5, f32[5,5,16,8,128]{4,3,2,1,0:T(8,128)} %jac_hbm.3, f32[5,3,5]{2,1,0:T(4,128)} %bitcast.5, f32[3,16,8,128]{3,2,1,0:T(8,128)} %face_hbm.3, f32[16,8,128]{2,1,0:T(8,128)} %kap_hbm.5, f32[5,16,8,128]{3,2,1,0:T(8,128)} %src_hbm.3, ...), custom_call_target="tpu_custom_call" | custom-call | tf_op jit(solution)/shard_map/sweep_inner/pallas_call | solution.py:404
  15.1 0.0 collective-permute-done.1.mate_ref
  15.1 0.0 collective-permute-done.2.other_ref
  15.1 3.8 %all-to-all-done = f32[8,2,8,256]{3,2,1,0:T(8,128)S(1)} async-done(((f32[8,2,8,256]{3,2,1,0:T(8,128)}), f32[8,2,8,256]{3,2,1,0:T(8,128)S(1)}, u32[]{:S(2)}, u32[]{:S(2)}) %all-to-all-start) | async-done | bytes 131104 | tf_op jit(solution)/shard_map/all_to_all | solution.py:401
  18.9 3.8 %sum_rows.1 = (f32[3,4096]{1,0:T(4,128)}, f32[5,16,8,128]{3,2,1,0:T(8,128)}) custom-call(f32[16,8,256]{2,1,0:T(8,128)S(1)} %bitcast.4, f32[5,16,8,128]{3,2,1,0:T(8,128)} %adj_hbm.5, f32[5,5,16,8,128]{4,3,2,1,0:T(8,128)} %jac_hbm.3, f32[5,3,5]{2,1,0:T(4,128)} %bitcast.6, f32[3,16,8,128]{3,2,1,0:T(8,128)} %face_hbm.3, ...), custom_call_target="tpu_custom_call", output_to_operand_aliasing={{1}: (9, {})} | custom-call | tf_op jit(solution)/shard_map/sum_rows/pallas_call | solution.py:424
Async XLA Ops:
  2.3 1.4 %collective-permute-start = (f32[8,8,256]{2,1,0:T(8,128)S(1)}, f32[8,8,256]{2,1,0:T(8,128)S(1)}, u32[]{:S(2)}, u32[]{:S(2)}) collective-permute-start(f32[8,8,256]{2,1,0:T(8,128)S(1)} %get-tuple-element.9), channel_id=1, source_target_pairs={{0,1},{1,0},{2,3},{3,2},{4,5},{5,4},{6,7},{7,6},{8,9},{9,8},{10,11... | collective-permute-start | bytes 196616 | tf_op jit(solution)/shard_map/ppermute | solution.py:388
  4.4 14.5 %all-to-all-start = ((f32[8,2,8,256]{3,2,1,0:T(8,128)}), f32[8,2,8,256]{3,2,1,0:T(8,128)S(1)}, u32[]{:S(2)}, u32[]{:S(2)}) async-start(f32[8,2,8,256]{3,2,1,0:T(8,128)} %merge_rows.1.after_hbm), calls=%async_computation | async-start | bytes 262144 | tf_op jit(solution)/shard_map/all_to_all | solution.py:401
  11.6 3.5 %collective-permute-start.1 = (f32[6,8,128]{2,1,0:T(8,128)S(1)}, f32[6,8,128]{2,1,0:T(8,128)S(1)}, u32[]{:S(2)}, u32[]{:S(2)}) collective-permute-start(f32[6,8,128]{2,1,0:T(8,128)S(1)} %get-tuple-element.10), channel_id=1, source_target_pairs={{0,1},{1,0},{2,3},{3,2},{4,5},{5,4},{6,7},{7,6},{8,9},{9,8},{10,11... | collective-permute-start | bytes 73736 | tf_op jit(solution)/shard_map/ppermute | solution.py:389
  11.6 3.5 %collective-permute-start.2 = (f32[6,8,128]{2,1,0:T(8,128)S(1)}, f32[6,8,128]{2,1,0:T(8,128)S(1)}, u32[]{:S(2)}, u32[]{:S(2)}) collective-permute-start(f32[6,8,128]{2,1,0:T(8,128)S(1)} %get-tuple-element.11), channel_id=1, source_target_pairs={{1,2},{2,1},{3,4},{4,3},{5,6},{6,5},{7,8},{8,7},{9,10},{10,9},{11,... | collective-permute-start | bytes 73736 | tf_op jit(solution)/shard_map/ppermute | solution.py:390

commit v2 on v0

--- a/solution.py
+++ b/solution.py
@@ -28,6 +28,19 @@
 
 def stay(*arrays):
     return [pltpu.with_memory_space_constraint(a, pltpu.HBM) for a in arrays]
+
+
+def spread(count):
+    quarter = count // 4
+    order = []
+    for k in range(quarter):
+        order += [
+            3 * quarter + k,
+            (k + 2) % quarter,
+            2 * quarter + (k + 3) % quarter,
+            quarter + (k + 1) % quarter,
+        ]
+    return order
 
 
 def start_all(copies):
@@ -120,7 +133,7 @@
         both = jnp.concatenate([hi, values - hi], 0)
         mine = box[:, part]
         lhs = jnp.concatenate(
-            [jnp.where(mine == b, both, 0.0) for b in range(boxes)], 0
+            [jnp.where(mine == b, both, 0.0) for b in spread(boxes)], 0
         ).astype(BF16)
         rhs = (slots == ranks_ref[:, part]).astype(F32).astype(BF16)
         total = total + lax.dot_general(lhs, rhs, NT, preferred_element_type=F32)
@@ -367,7 +380,7 @@
         compiler_params=params,
         name="pack_rows",
     )(adjoint, kappa, box_row, cell_row, lattice_frac, dres_dx, dobj_dx)
-    got = lax.all_to_all(packed, "blk", 0, 0, tiled=True)
+    got = lax.all_to_all(packed, "blk", 0, 0, axis_index_groups=[spread(boxes)], tiled=True)
 
     pairs = [(i, i + 1) for i in range(boxes - 1)]
     both_ways = [[p for i, j in pairs if i % 2 == turn for p in ((i, j), (j, i))] for turn in (0, 1)]

time: 22.4 us -> 21.8 us (0.973)
  waiting for transfers between devices: 1.08 us -> 0.01 us
  starting transfers between devices: 11.4 us -> 11.9 us
    all_to_all x1, waiting for transfers between devices: 1.07 us -> 0.01 us  [local(): lax.all_to_all(packed, 'blk', 0, 0, axis_index_groups=[spread(boxes)], ti...]
    all_to_all x1, starting transfers between devices: 7.4 us -> 8.41 us  [local(): lax.all_to_all(packed, 'blk', 0, 0, axis_index_groups=[spread(boxes)], ti...]
    ppermute x1, starting transfers between devices: 3.34 us -> 2.83 us  [local(): mate = lax.ppermute(to_mate, 'blk', both_ways[0])]
  transfers between devices with their start and end apart: 3 -> 3, of which waited for: 1 -> 0; matrix products, arithmetic and copies ran while one was open for 0% -> 0% of each run, Pallas kernels for 13% -> 13%
where the time goes in v2:
time: 21.8 us; the launch traced here: 21.5 us
  starting transfers between devices  11.9 us (55%)
  Pallas kernels  8.93 us (41%)
  between operations  0.68 us (3%)
    all_to_all x1, starting transfers between devices, local(): lax.all_to_all(packed, 'blk', 0, 0, axis_index_groups=[spread(boxes)], ti...  8.41 us
    pallas_call x1, Pallas kernels, local(): pl.pallas_call(sum_kernel, out_shape=(shape(3, LAT ** 3), shape(*adjoint....  3.78 us
    ppermute x1, starting transfers between devices, local(): mate = lax.ppermute(to_mate, 'blk', both_ways[0])  2.83 us
    pallas_call x1, Pallas kernels, local(): pl.pallas_call(inner_kernel, out_shape=shape(*adjoint.shape), in_specs=[h...  2.82 us
    pallas_call x1, Pallas kernels, local(): pl.pallas_call(functools.partial(pack_kernel, boxes, cap), out_shape=(sha...  2.33 us
    ppermute x1, starting transfers between devices, local(): other = lax.ppermute(to_other, 'blk', both_ways[1])  0.65 us
  transfers between devices with their start and end apart: 3, of which 0 were waited for; matrix products, arithmetic and copies ran while one was open for 0% of the time, Pallas kernels for 13%

profile of v2, /device:TPU:0, one launch (start us, length us, event | category | flops | bytes accessed | tf_op | source)
XLA Modules:
  0.0 21.5 jit_solution(15493383785808996225)
XLA Ops:
  0.6 2.3 %pack_rows.1 = (f32[16,8,256]{2,1,0:T(8,128)}, f32[6,8,128]{2,1,0:T(8,128)S(1)}, f32[6,8,128]{2,1,0:T(8,128)S(1)}) custom-call(f32[5,16,8,128]{3,2,1,0:T(8,128)} %adj_hbm.5, f32[16,8,128]{2,1,0:T(8,128)} %kap_hbm.5, s32[1,2048]{1,0:T(1,128)} %bitcast.5, s32[1,2048]{1,0:T(1,128)} %bitcast.6, f32[3,2048]{1,0:T(4,128)} %frac_hbm.1, f32[5,3,2048]{2,1,0:T(4,128)} %dres_hbm.1, ...), custom_call_target="tpu_custom_call" | custom-call | tf_op jit(solution)/shard_map/pack_rows/pallas_call | solution.py:364
  3.0 8.4 %all-to-all-start = ((f32[16,8,256]{2,1,0:T(8,128)}), f32[16,8,256]{2,1,0:T(8,128)S(1)}, u32[]{:S(2)}, u32[]{:S(2)}) async-start(f32[16,8,256]{2,1,0:T(8,128)} %get-tuple-element.7), calls=%async_computation | async-start | bytes 262144 | tf_op jit(solution)/shard_map/all_to_all | solution.py:383
  11.4 0.7 %collective-permute-start.1 = (f32[6,8,128]{2,1,0:T(8,128)S(1)}, f32[6,8,128]{2,1,0:T(8,128)S(1)}, u32[]{:S(2)}, u32[]{:S(2)}) collective-permute-start(f32[6,8,128]{2,1,0:T(8,128)S(1)} %get-tuple-element.9), channel_id=1, source_target_pairs={{1,2},{2,1},{3,4},{4,3},{5,6},{6,5},{7,8},{8,7},{9,10},{10,9},{11,... | collective-permute-start | bytes 73736 | tf_op jit(solution)/shard_map/ppermute | solution.py:388
  12.0 2.8 %collective-permute-start = (f32[6,8,128]{2,1,0:T(8,128)S(1)}, f32[6,8,128]{2,1,0:T(8,128)S(1)}, u32[]{:S(2)}, u32[]{:S(2)}) collective-permute-start(f32[6,8,128]{2,1,0:T(8,128)S(1)} %get-tuple-element.8.after_hbm), channel_id=1, source_target_pairs={{0,1},{1,0},{2,3},{3,2},{4,5},{5,4},{6,7},{7,6},{8,9},{9,8},{10,11... | collective-permute-start | bytes 73736 | tf_op jit(solution)/shard_map/ppermute | solution.py:387
  14.9 2.8 %sweep_inner.1.part_hbm = f32[5,16,8,128]{3,2,1,0:T(8,128)} custom-call(f32[5,16,8,128]{3,2,1,0:T(8,128)} %adj_hbm.5, f32[5,5,16,8,128]{4,3,2,1,0:T(8,128)} %jac_hbm.3, f32[5,3,5]{2,1,0:T(4,128)} %bitcast.3, f32[3,16,8,128]{3,2,1,0:T(8,128)} %face_hbm.3, f32[16,8,128]{2,1,0:T(8,128)} %kap_hbm.5, f32[5,16,8,128]{3,2,1,0:T(8,128)} %src_hbm.3, ...), custom_call_target="tpu_custom_call" | custom-call | tf_op jit(solution)/shard_map/sweep_inner/pallas_call | solution.py:390
  17.7 0.0 collective-permute-done.1.other_ref
  17.7 0.0 collective-permute-done.mate_ref
  17.7 0.0 all-to-all-done.got_ref
  17.7 3.8 %sum_rows.1 = (f32[3,4096]{1,0:T(4,128)}, f32[5,16,8,128]{3,2,1,0:T(8,128)}) custom-call(f32[16,8,256]{2,1,0:T(8,128)S(1)} %all-to-all-done.got_ref, f32[5,16,8,128]{3,2,1,0:T(8,128)} %adj_hbm.5, f32[5,5,16,8,128]{4,3,2,1,0:T(8,128)} %jac_hbm.3, f32[5,3,5]{2,1,0:T(4,128)} %bitcast.4, f32[3,16,8,128]{3,2,1,0:T(8,128)} %face_hbm.3, ...), custom_call_target="tpu_custom_call", output_to_operand_aliasing={{1}: (9, {})} | custom-call | tf_op jit(solution)/shard_map/sum_rows/pallas_call | solution.py:410
Async XLA Ops:
  3.0 14.8 %all-to-all-start = ((f32[16,8,256]{2,1,0:T(8,128)}), f32[16,8,256]{2,1,0:T(8,128)S(1)}, u32[]{:S(2)}, u32[]{:S(2)}) async-start(f32[16,8,256]{2,1,0:T(8,128)} %get-tuple-element.7), calls=%async_computation | async-start | bytes 262144 | tf_op jit(solution)/shard_map/all_to_all | solution.py:383
  11.4 6.3 %collective-permute-start.1 = (f32[6,8,128]{2,1,0:T(8,128)S(1)}, f32[6,8,128]{2,1,0:T(8,128)S(1)}, u32[]{:S(2)}, u32[]{:S(2)}) collective-permute-start(f32[6,8,128]{2,1,0:T(8,128)S(1)} %get-tuple-element.9), channel_id=1, source_target_pairs={{1,2},{2,1},{3,4},{4,3},{5,6},{6,5},{7,8},{8,7},{9,10},{10,9},{11,... | collective-permute-start | bytes 73736 | tf_op jit(solution)/shard_map/ppermute | solution.py:388
  12.0 5.7 %collective-permute-start = (f32[6,8,128]{2,1,0:T(8,128)S(1)}, f32[6,8,128]{2,1,0:T(8,128)S(1)}, u32[]{:S(2)}, u32[]{:S(2)}) collective-permute-start(f32[6,8,128]{2,1,0:T(8,128)S(1)} %get-tuple-element.8.after_hbm), channel_id=1, source_target_pairs={{0,1},{1,0},{2,3},{3,2},{4,5},{5,4},{6,7},{7,6},{8,9},{9,8},{10,11... | collective-permute-start | bytes 73736 | tf_op jit(solution)/shard_map/ppermute | solution.py:387

commit v3 on v2

--- a/solution.py
+++ b/solution.py
@@ -9,6 +9,7 @@
 
 LAT = 16
 CHUNK = 256
+ROW = 7
 SMALL = 12 * 2**20
 F32 = jnp.float32
 BF16 = jnp.bfloat16
@@ -35,10 +36,10 @@
     order = []
     for k in range(quarter):
         order += [
-            3 * quarter + k,
-            (k + 2) % quarter,
-            2 * quarter + (k + 3) % quarter,
-            quarter + (k + 1) % quarter,
+            quarter + k,
+            3 * quarter + (k + 2) % quarter,
+            (k + 3) % quarter,
+            2 * quarter + (k + 1) % quarter,
         ]
     return order
 
@@ -137,8 +138,11 @@
         ).astype(BF16)
         rhs = (slots == ranks_ref[:, part]).astype(F32).astype(BF16)
         total = total + lax.dot_general(lhs, rhs, NT, preferred_element_type=F32)
+    width = out_ref.shape[-1]
     for b in range(boxes):
-        out_ref[b] = total[b * 16:b * 16 + 8] + total[b * 16 + 8:b * 16 + 16]
+        block = total[b * 16:b * 16 + ROW] + total[b * 16 + 8:b * 16 + 8 + ROW]
+        for i in range(cap // width):
+            out_ref[b, :, i, :] = block[:, i * width:(i + 1) * width]
 
 
 def plane_residual(psi, kap, below, above, jac, face, src, conv):
@@ -177,7 +181,7 @@
     return [result[f] + spread * psi[f] for f in range(fields)]
 
 
-def inner_kernel(
+def sweep_kernel(
     adj_hbm,
     jac_hbm,
     conv_hbm,
@@ -186,6 +190,7 @@
     src_hbm,
     after_hbm,
     out_hbm,
+    edge_ref,
     adj_ref,
     jac_ref,
     conv_ref,
@@ -198,7 +203,7 @@
 ):
     fields, planes, _, _ = adj_hbm.shape
     steps = 4
-    cuts = [1 + (planes - 2) * i // steps for i in range(steps + 1)]
+    cuts = [planes * i // steps for i in range(steps + 1)]
     pieces = [slice(a, b) for a, b in zip(cuts[:-1], cuts[1:])]
     moves = [(adj_hbm, adj_ref), (kap_hbm, kap_ref), (conv_hbm, conv_ref)]
     for p in pieces:
@@ -209,12 +214,15 @@
         [pltpu.make_async_copy(src, dst, sems.at[i]) for i, (src, dst) in enumerate(moves)]
     )
     wait_all(copies[:3])
+    nothing = [jnp.zeros(adj_hbm.shape[2:], F32)] * (fields + 1)
     sent = []
     for i, p in enumerate(pieces):
         wait_all(copies[3 + 3 * i:6 + 3 * i])
         for x in range(p.start, p.stop):
             def at(y):
-                return [adj_ref[f, y] for f in range(fields)] + [kap_ref[y]]
+                if 0 <= y < planes:
+                    return [adj_ref[f, y] for f in range(fields)] + [kap_ref[y]]
+                return nothing
 
             here = at(x)
             planes_of = plane_residual(
@@ -229,6 +237,13 @@
             )
             for f in range(fields):
                 out_ref[f, x] = planes_of[f]
+            if x in (0, planes - 1):
+                e = 0 if x == 0 else 1
+                for f in range(fields):
+                    edge_ref[e, f] = planes_of[f]
+                    edge_ref[e, fields + f] = here[f]
+                edge_ref[e, 2 * fields] = here[fields]
+                edge_ref[e, 2 * fields + 1] = face_ref[0, x]
         copy = pltpu.make_async_copy(out_ref.at[:, p], out_hbm.at[:, p], out_sems.at[i])
         copy.start()
         sent.append(copy)
@@ -237,48 +252,55 @@
 
 def sum_kernel(
     got_ref,
-    adj_hbm,
-    jac_hbm,
-    conv_hbm,
-    face_hbm,
-    kap_hbm,
-    src_hbm,
+    edge_ref,
     mate_ref,
     other_ref,
+    conv_hbm,
     part_hbm,
     out_ref,
     res_hbm,
-    adj_ref,
-    jac_ref,
     conv_ref,
-    face_ref,
-    kap_ref,
-    src_ref,
     res_ref,
-    sems,
+    sem,
     out_sems,
 ):
     del part_hbm
-    fields, planes, _, _ = adj_hbm.shape
-    ends = (0, planes - 1)
-    moves = [(conv_hbm, conv_ref)]
-    for i, x in enumerate(ends):
-        near = pl.ds(0 if i == 0 else planes - 2, 2)
-        moves.append((adj_hbm.at[:, near], adj_ref.at[i]))
-        moves.append((kap_hbm.at[near], kap_ref.at[i]))
-        moves.append((jac_hbm.at[:, :, x], jac_ref.at[i]))
-        moves.append((src_hbm.at[:, x], src_ref.at[i]))
-        moves.append((face_hbm.at[:, x], face_ref.at[i]))
-    copies = start_all(
-        [pltpu.make_async_copy(src, dst, sems.at[i]) for i, (src, dst) in enumerate(moves)]
-    )
-
-    sources, _, cap = got_ref.shape
+    fields, planes = res_hbm.shape[:2]
+    conv_copy = pltpu.make_async_copy(conv_hbm, conv_ref, sem)
+    conv_copy.start()
+
+    def edges():
+        conv_copy.wait()
+        even = on_even()
+        copies = []
+        for e in (0, 1):
+            beyond = [
+                jnp.where(even == (e == 0), other_ref[f], mate_ref[f]) for f in range(fields + 1)
+            ]
+            kap = edge_ref[e, 2 * fields]
+            scale = edge_ref[e, 2 * fields + 1] * (0.5 if e else -0.5)
+            terms = [scale * beyond[k] for k in range(fields)]
+            weight = 0.5 * (kap + beyond[fields])
+            extra = 0.5 * beyond[fields]
+            for f in range(fields):
+                total = edge_ref[e, f] - weight * beyond[f] + extra * edge_ref[e, fields + f]
+                for k in range(fields):
+                    total = total + conv_ref[k, 0, f] * terms[k]
+                res_ref[e, f] = total
+            copies.append(
+                pltpu.make_async_copy(res_ref.at[e], res_hbm.at[:, e * (planes - 1)], out_sems.at[e])
+            )
+        return start_all(copies)
+
+    sources, _, cuts, width = got_ref.shape
+    cap = cuts * width
     inner = LAT - 1
     points = lax.broadcasted_iota(jnp.int32, (LAT, cap), 0).astype(F32)
     both = jnp.zeros((6 * LAT, LAT * LAT), F32)
     for s in range(sources):
-        block = got_ref[s]
+        if s == sources // 2:
+            sent = edges()
+        block = jnp.concatenate([got_ref[s, :, i, :] for i in range(cuts)], 1)
         cell = block[6:7]
         first = jnp.floor((cell + 0.5) * (1.0 / (inner * inner)))
         rest = cell - first * (inner * inner)
@@ -297,31 +319,6 @@
         lhs = jnp.concatenate([left_hi, left_lo], 0)
         both = both + lax.dot_general(lhs, right_hi, NT, preferred_element_type=F32)
         both = both + lax.dot_general(lhs, right_lo, NT, preferred_element_type=F32)
-
-    wait_all(copies)
-    even = on_even()
-    sent = []
-    for i, x in enumerate(ends):
-        pair = [[adj_ref[i, f, j] for f in range(fields)] + [kap_ref[i, j]] for j in (0, 1)]
-        beyond = [
-            jnp.where(even == (i == 0), other_ref[f], mate_ref[f]) for f in range(fields + 1)
-        ]
-        here = pair[i]
-        planes_of = plane_residual(
-            here[:fields],
-            here[fields],
-            beyond if i == 0 else pair[0],
-            pair[1] if i == 0 else beyond,
-            lambda k, f: jac_ref[i, k, f],
-            lambda d: face_ref[i, d],
-            lambda f: src_ref[i, f],
-            conv_ref,
-        )
-        for f in range(fields):
-            res_ref[i, f] = planes_of[f]
-        copy = pltpu.make_async_copy(res_ref.at[i], res_hbm.at[:, x], out_sems.at[i])
-        copy.start()
-        sent.append(copy)
     result = both[:3 * LAT] + both[3 * LAT:]
     for c in range(3):
         for a in range(LAT):
@@ -358,12 +355,15 @@
     )
     lattice_frac, dres_dx, dobj_dx = stay(lattice_frac, dres_dx, dobj_dx)
 
+    width = min(128, cap)
+    payload = (boxes, ROW, cap // width, width)
+
     def shape(*dims):
         return jax.ShapeDtypeStruct(dims, F32)
 
     packed, to_mate, to_other = pl.pallas_call(
         functools.partial(pack_kernel, boxes, cap),
-        out_shape=(shape(boxes, 8, cap), shape(fields + 1, *plane), shape(fields + 1, *plane)),
+        out_shape=(shape(*payload), shape(fields + 1, *plane), shape(fields + 1, *plane)),
         in_specs=[hbm] * 7,
         out_specs=(vmem, vmem, vmem),
         scratch_shapes=[
@@ -387,11 +387,11 @@
     mate = lax.ppermute(to_mate, "blk", both_ways[0])
     other = lax.ppermute(to_other, "blk", both_ways[1])
 
-    inner = pl.pallas_call(
-        inner_kernel,
-        out_shape=shape(*adjoint.shape),
+    inner, edge = pl.pallas_call(
+        sweep_kernel,
+        out_shape=(shape(*adjoint.shape), shape(2, 2 * fields + 2, *plane)),
         in_specs=[hbm] * 6 + [pl.BlockSpec(memory_space=pl.ANY)],
-        out_specs=hbm,
+        out_specs=(hbm, vmem),
         scratch_shapes=[
             pltpu.VMEM(adjoint.shape, F32),
             pltpu.VMEM(jac_diag.shape, F32),
@@ -404,29 +404,24 @@
             pltpu.SemaphoreType.DMA((4,)),
         ],
         compiler_params=params,
-        name="sweep_inner",
+        name="sweep_planes",
     )(adjoint, jac_diag, conv, face_scale, kappa, source, to_mate)
 
     box_sens, residual = pl.pallas_call(
         sum_kernel,
         out_shape=(shape(3, LAT**3), shape(*adjoint.shape)),
-        in_specs=[vmem] + [hbm] * 6 + [vmem, vmem, hbm],
+        in_specs=[vmem] * 4 + [hbm, hbm],
         out_specs=(vmem, hbm),
         scratch_shapes=[
-            pltpu.VMEM((2, fields, 2) + plane, F32),
-            pltpu.VMEM((2, fields, fields) + plane, F32),
             pltpu.SMEM(conv.shape, F32),
-            pltpu.VMEM((2, 3) + plane, F32),
-            pltpu.VMEM((2, 2) + plane, F32),
             pltpu.VMEM((2, fields) + plane, F32),
-            pltpu.VMEM((2, fields) + plane, F32),
-            pltpu.SemaphoreType.DMA((11,)),
+            pltpu.SemaphoreType.DMA,
             pltpu.SemaphoreType.DMA((2,)),
         ],
-        input_output_aliases={9: 1},
+        input_output_aliases={5: 1},
         compiler_params=params,
         name="sum_rows",
-    )(got, adjoint, jac_diag, conv, face_scale, kappa, source, mate, other, inner)
+    )(got, edge, mate, other, conv, inner)
     return residual, box_sens
 
 

time: 21.8 us -> 21.6 us (level)
  starting transfers between devices: 11.9 us -> 11.4 us
    all_to_all x1, starting transfers between devices: 8.41 us -> 7.87 us  [local(): lax.all_to_all(packed, 'blk', 0, 0, axis_index_groups=[spread(boxes)], ti...]
  transfers between devices with their start and end apart: 3 -> 3, of which waited for: 0 -> 0; matrix products, arithmetic and copies ran while one was open for 0% -> 0% of each run, Pallas kernels for 13% -> 14%
where the time goes in v3:
time: 21.6 us; the launch traced here: 21.3 us
  starting transfers between devices  11.4 us (53%)
  Pallas kernels  9.13 us (42%)
  between operations  0.68 us (3%)
    all_to_all x1, starting transfers between devices, local(): lax.all_to_all(packed, 'blk', 0, 0, axis_index_groups=[spread(boxes)], ti...  7.87 us
    pallas_call x1, Pallas kernels, local(): pl.pallas_call(sum_kernel, out_shape=(shape(3, LAT ** 3), shape(*adjoint....  3.8 us
    pallas_call x1, Pallas kernels, local(): pl.pallas_call(sweep_kernel, out_shape=(shape(*adjoint.shape), shape(2, 2...  2.99 us
    ppermute x1, starting transfers between devices, local(): mate = lax.ppermute(to_mate, 'blk', both_ways[0])  2.92 us
    pallas_call x1, Pallas kernels, local(): pl.pallas_call(functools.partial(pack_kernel, boxes, cap), out_shape=(sha...  2.34 us
    ppermute x1, starting transfers between devices, local(): other = lax.ppermute(to_other, 'blk', both_ways[1])  0.65 us
  transfers between devices with their start and end apart: 3, of which 0 were waited for; matrix products, arithmetic and copies ran while one was open for 0% of the time, Pallas kernels for 14%

profile of v3, /device:TPU:0, one launch (start us, length us, event | category | flops | bytes accessed | tf_op | source)
XLA Modules:
  0.0 21.3 jit_solution(4805175358839128303)
XLA Ops:
  0.6 2.3 %pack_rows.1 = (f32[16,7,2,128]{3,2,1,0:T(2,128)}, f32[6,8,128]{2,1,0:T(8,128)S(1)}, f32[6,8,128]{2,1,0:T(8,128)S(1)}) custom-call(f32[5,16,8,128]{3,2,1,0:T(8,128)} %adj_hbm.3, f32[16,8,128]{2,1,0:T(8,128)} %kap_hbm.3, s32[1,2048]{1,0:T(1,128)} %bitcast.5, s32[1,2048]{1,0:T(1,128)} %bitcast.6, f32[3,2048]{1,0:T(4,128)} %frac_hbm.1, f32[5,3,2048]{2,1,0:T(4,128)} %dres_hbm.1, ...), custom_call_target="tpu_custom_call" | custom-call | tf_op jit(solution)/shard_map/pack_rows/pallas_call | solution.py:364
  3.0 7.9 %all-to-all-start = ((f32[16,7,2,128]{3,2,1,0:T(2,128)}), f32[16,7,2,128]{3,2,1,0:T(2,128)S(1)}, u32[]{:S(2)}, u32[]{:S(2)}) async-start(f32[16,7,2,128]{3,2,1,0:T(2,128)} %get-tuple-element.9), calls=%async_computation | async-start | bytes 229376 | tf_op jit(solution)/shard_map/all_to_all | solution.py:383
  10.8 0.7 %collective-permute-start.1 = (f32[6,8,128]{2,1,0:T(8,128)S(1)}, f32[6,8,128]{2,1,0:T(8,128)S(1)}, u32[]{:S(2)}, u32[]{:S(2)}) collective-permute-start(f32[6,8,128]{2,1,0:T(8,128)S(1)} %get-tuple-element.12), channel_id=1, source_target_pairs={{1,2},{2,1},{3,4},{4,3},{5,6},{6,5},{7,8},{8,7},{9,10},{10,9},{11,... | collective-permute-start | bytes 73736 | tf_op jit(solution)/shard_map/ppermute | solution.py:388
  11.5 2.9 %collective-permute-start = (f32[6,8,128]{2,1,0:T(8,128)S(1)}, f32[6,8,128]{2,1,0:T(8,128)S(1)}, u32[]{:S(2)}, u32[]{:S(2)}) collective-permute-start(f32[6,8,128]{2,1,0:T(8,128)S(1)} %get-tuple-element.10.after_hbm), channel_id=1, source_target_pairs={{0,1},{1,0},{2,3},{3,2},{4,5},{5,4},{6,7},{7,6},{8,9},{9,8},{10,11... | collective-permute-start | bytes 73736 | tf_op jit(solution)/shard_map/ppermute | solution.py:387
  14.4 3.0 %sweep_planes.1 = (f32[5,16,8,128]{3,2,1,0:T(8,128)}, f32[2,12,8,128]{3,2,1,0:T(8,128)S(1)}) custom-call(f32[5,16,8,128]{3,2,1,0:T(8,128)} %adj_hbm.3, f32[5,5,16,8,128]{4,3,2,1,0:T(8,128)} %jac_hbm.1, f32[5,3,5]{2,1,0:T(4,128)} %bitcast.3, f32[3,16,8,128]{3,2,1,0:T(8,128)} %face_hbm.1, f32[16,8,128]{2,1,0:T(8,128)} %kap_hbm.3, f32[5,16,8,128]{3,2,1,0:T(8,128)} %src_hbm.1, ...), custom_call_target="tpu_custom_call" | custom-call | tf_op jit(solution)/shard_map/sweep_planes/pallas_call | solution.py:390
  17.4 0.0 collective-permute-done.1.other_ref
  17.4 0.0 collective-permute-done.mate_ref
  17.4 0.0 all-to-all-done.got_ref
  17.5 3.8 %sum_rows.1 = (f32[3,4096]{1,0:T(4,128)}, f32[5,16,8,128]{3,2,1,0:T(8,128)}) custom-call(f32[16,7,2,128]{3,2,1,0:T(2,128)S(1)} %all-to-all-done.got_ref, f32[2,12,8,128]{3,2,1,0:T(8,128)S(1)} %get-tuple-element.11.edge_ref, f32[6,8,128]{2,1,0:T(8,128)S(1)} %collective-permute-done.mate_ref, ...), custom_call_target="tpu_custom_call", output_to_operand_aliasing={{1}: (5, {})} | custom-call | tf_op jit(solution)/shard_map/sum_rows/pallas_call | solution.py:410
Async XLA Ops:
  3.0 14.5 %all-to-all-start = ((f32[16,7,2,128]{3,2,1,0:T(2,128)}), f32[16,7,2,128]{3,2,1,0:T(2,128)S(1)}, u32[]{:S(2)}, u32[]{:S(2)}) async-start(f32[16,7,2,128]{3,2,1,0:T(2,128)} %get-tuple-element.9), calls=%async_computation | async-start | bytes 229376 | tf_op jit(solution)/shard_map/all_to_all | solution.py:383
  10.8 6.6 %collective-permute-start.1 = (f32[6,8,128]{2,1,0:T(8,128)S(1)}, f32[6,8,128]{2,1,0:T(8,128)S(1)}, u32[]{:S(2)}, u32[]{:S(2)}) collective-permute-start(f32[6,8,128]{2,1,0:T(8,128)S(1)} %get-tuple-element.12), channel_id=1, source_target_pairs={{1,2},{2,1},{3,4},{4,3},{5,6},{6,5},{7,8},{8,7},{9,10},{10,9},{11,... | collective-permute-start | bytes 73736 | tf_op jit(solution)/shard_map/ppermute | solution.py:388
  11.5 5.9 %collective-permute-start = (f32[6,8,128]{2,1,0:T(8,128)S(1)}, f32[6,8,128]{2,1,0:T(8,128)S(1)}, u32[]{:S(2)}, u32[]{:S(2)}) collective-permute-start(f32[6,8,128]{2,1,0:T(8,128)S(1)} %get-tuple-element.10.after_hbm), channel_id=1, source_target_pairs={{0,1},{1,0},{2,3},{3,2},{4,5},{5,4},{6,7},{7,6},{8,9},{9,8},{10,11... | collective-permute-start | bytes 73736 | tf_op jit(solution)/shard_map/ppermute | solution.py:387

commit v4 on v3

--- a/solution.py
+++ b/solution.py
@@ -65,11 +65,20 @@
     frac_hbm,
     dres_hbm,
     dobj_hbm,
+    conv_hbm,
+    jac_hbm,
+    src_hbm,
+    face_hbm,
     out_ref,
     mate_ref,
     other_ref,
     adj_ref,
     kap_ref,
+    fill_ref,
+    jac_ref,
+    src_ref,
+    face_ref,
+    conv_ref,
     box_ref,
     cell_ref,
     frac_ref,
@@ -80,10 +89,10 @@
 ):
     fields, planes, _, lanes = adj_hbm.shape
     rows = planes * lanes
-    ends = (0, planes - 1)
     moves = [(box_hbm, box_ref), (dres_hbm, dres_ref), (adj_hbm, adj_ref)]
     moves += [(dobj_hbm, dobj_ref), (frac_hbm, frac_ref), (cell_hbm, cell_ref)]
-    moves += [(kap_hbm.at[x], kap_ref.at[i]) for i, x in enumerate(ends)]
+    moves += [(kap_hbm, kap_ref), (conv_hbm, conv_ref), (jac_hbm, jac_ref)]
+    moves += [(src_hbm, src_ref), (face_hbm, face_ref)]
     copies = start_all(
         [pltpu.make_async_copy(src, dst, sems.at[i]) for i, (src, dst) in enumerate(moves)]
     )
@@ -108,11 +117,11 @@
         )
         offset = offset + here[:, CHUNK - 1:] + hot[j][:, CHUNK - 1:]
 
-    wait_all(copies[1:])
+    wait_all(copies[1:7])
     even = on_even()
     for f in range(fields + 1):
         first = adj_ref[f, 0] if f < fields else kap_ref[0]
-        last = adj_ref[f, planes - 1] if f < fields else kap_ref[1]
+        last = adj_ref[f, planes - 1] if f < fields else kap_ref[planes - 1]
         mate_ref[f] = jnp.where(even, last, first)
         other_ref[f] = jnp.where(even, first, last)
 
@@ -143,6 +152,11 @@
         block = total[b * 16:b * 16 + ROW] + total[b * 16 + 8:b * 16 + 8 + ROW]
         for i in range(cap // width):
             out_ref[b, :, i, :] = block[:, i * width:(i + 1) * width]
+    wait_all(copies[7:])
+    for k in range(fields):
+        for d in range(3):
+            for f in range(fields):
+                fill_ref[k, d, f] = jnp.full(kap_ref.shape[1:], conv_ref[k, d, f], F32)
 
 
 def plane_residual(psi, kap, below, above, jac, face, src, conv):
@@ -176,48 +190,30 @@
         for f in range(fields):
             total = result[f]
             for k in range(fields):
-                total = total + conv[k, d, f] * diff[k]
+                total = total + conv(k, d, f) * diff[k]
             result[f] = total - up * pair[f][0] - down * pair[f][1]
     return [result[f] + spread * psi[f] for f in range(fields)]
 
 
 def sweep_kernel(
-    adj_hbm,
-    jac_hbm,
-    conv_hbm,
-    face_hbm,
-    kap_hbm,
-    src_hbm,
-    after_hbm,
-    out_hbm,
-    edge_ref,
     adj_ref,
     jac_ref,
-    conv_ref,
+    fill_ref,
     face_ref,
     kap_ref,
     src_ref,
+    out_hbm,
+    edge_ref,
     out_ref,
-    sems,
     out_sems,
 ):
-    fields, planes, _, _ = adj_hbm.shape
+    fields, planes = adj_ref.shape[:2]
     steps = 4
     cuts = [planes * i // steps for i in range(steps + 1)]
     pieces = [slice(a, b) for a, b in zip(cuts[:-1], cuts[1:])]
-    moves = [(adj_hbm, adj_ref), (kap_hbm, kap_ref), (conv_hbm, conv_ref)]
-    for p in pieces:
-        moves.append((jac_hbm.at[:, :, p], jac_ref.at[:, :, p]))
-        moves.append((src_hbm.at[:, p], src_ref.at[:, p]))
-        moves.append((face_hbm.at[:, p], face_ref.at[:, p]))
-    copies = start_all(
-        [pltpu.make_async_copy(src, dst, sems.at[i]) for i, (src, dst) in enumerate(moves)]
-    )
-    wait_all(copies[:3])
-    nothing = [jnp.zeros(adj_hbm.shape[2:], F32)] * (fields + 1)
+    nothing = [jnp.zeros(kap_ref.shape[1:], F32)] * (fields + 1)
     sent = []
     for i, p in enumerate(pieces):
-        wait_all(copies[3 + 3 * i:6 + 3 * i])
         for x in range(p.start, p.stop):
             def at(y):
                 if 0 <= y < planes:
@@ -233,20 +229,23 @@
                 lambda k, f: jac_ref[k, f, x],
                 lambda d: face_ref[d, x],
                 lambda f: src_ref[f, x],
-                conv_ref,
+                lambda k, d, f: fill_ref[k, d, f],
             )
             for f in range(fields):
                 out_ref[f, x] = planes_of[f]
             if x in (0, planes - 1):
-                e = 0 if x == 0 else 1
+                e = 0 if x == 0 else 2 * fields + 2
                 for f in range(fields):
-                    edge_ref[e, f] = planes_of[f]
-                    edge_ref[e, fields + f] = here[f]
-                edge_ref[e, 2 * fields] = here[fields]
-                edge_ref[e, 2 * fields + 1] = face_ref[0, x]
+                    edge_ref[e + f] = planes_of[f]
+                    edge_ref[e + fields + f] = here[f]
+                edge_ref[e + 2 * fields] = here[fields]
+                edge_ref[e + 2 * fields + 1] = face_ref[0, x]
         copy = pltpu.make_async_copy(out_ref.at[:, p], out_hbm.at[:, p], out_sems.at[i])
         copy.start()
         sent.append(copy)
+    for k in range(fields):
+        for f in range(fields):
+            edge_ref[4 * fields + 4 + k * fields + f] = fill_ref[k, 0, f]
     wait_all(sent)
 
 
@@ -255,37 +254,32 @@
     edge_ref,
     mate_ref,
     other_ref,
-    conv_hbm,
     part_hbm,
     out_ref,
     res_hbm,
-    conv_ref,
     res_ref,
-    sem,
     out_sems,
 ):
     del part_hbm
     fields, planes = res_hbm.shape[:2]
-    conv_copy = pltpu.make_async_copy(conv_hbm, conv_ref, sem)
-    conv_copy.start()
 
     def edges():
-        conv_copy.wait()
         even = on_even()
         copies = []
         for e in (0, 1):
             beyond = [
                 jnp.where(even == (e == 0), other_ref[f], mate_ref[f]) for f in range(fields + 1)
             ]
-            kap = edge_ref[e, 2 * fields]
-            scale = edge_ref[e, 2 * fields + 1] * (0.5 if e else -0.5)
+            base = e * (2 * fields + 2)
+            kap = edge_ref[base + 2 * fields]
+            scale = edge_ref[base + 2 * fields + 1] * (0.5 if e else -0.5)
             terms = [scale * beyond[k] for k in range(fields)]
             weight = 0.5 * (kap + beyond[fields])
             extra = 0.5 * beyond[fields]
             for f in range(fields):
-                total = edge_ref[e, f] - weight * beyond[f] + extra * edge_ref[e, fields + f]
+                total = edge_ref[base + f] - weight * beyond[f] + extra * edge_ref[base + fields + f]
                 for k in range(fields):
-                    total = total + conv_ref[k, 0, f] * terms[k]
+                    total = total + edge_ref[4 * fields + 4 + k * fields + f] * terms[k]
                 res_ref[e, f] = total
             copies.append(
                 pltpu.make_async_copy(res_ref.at[e], res_hbm.at[:, e * (planes - 1)], out_sems.at[e])
@@ -298,7 +292,7 @@
     points = lax.broadcasted_iota(jnp.int32, (LAT, cap), 0).astype(F32)
     both = jnp.zeros((6 * LAT, LAT * LAT), F32)
     for s in range(sources):
-        if s == sources // 2:
+        if s == sources // 4:
             sent = edges()
         block = jnp.concatenate([got_ref[s, :, i, :] for i in range(cuts)], 1)
         cell = block[6:7]
@@ -361,25 +355,47 @@
     def shape(*dims):
         return jax.ShapeDtypeStruct(dims, F32)
 
-    packed, to_mate, to_other = pl.pallas_call(
+    halo = shape(fields + 1, *plane)
+    packed, to_mate, to_other, adj, kap, fill, jac, src, face = pl.pallas_call(
         functools.partial(pack_kernel, boxes, cap),
-        out_shape=(shape(*payload), shape(fields + 1, *plane), shape(fields + 1, *plane)),
-        in_specs=[hbm] * 7,
-        out_specs=(vmem, vmem, vmem),
+        out_shape=(
+            shape(*payload),
+            halo,
+            halo,
+            shape(*adjoint.shape),
+            shape(*kappa.shape),
+            shape(*conv.shape, *plane),
+            shape(*jac_diag.shape),
+            shape(*source.shape),
+            shape(*face_scale.shape),
+        ),
+        in_specs=[hbm] * 11,
+        out_specs=(vmem,) * 9,
         scratch_shapes=[
-            pltpu.VMEM(adjoint.shape, F32),
-            pltpu.VMEM((2,) + plane, F32),
+            pltpu.SMEM(conv.shape, F32),
             pltpu.VMEM((1, rows), jnp.int32),
             pltpu.VMEM((1, rows), jnp.int32),
             pltpu.VMEM(lattice_frac.shape, F32),
             pltpu.VMEM(dres_dx.shape, F32),
             pltpu.VMEM(dobj_dx.shape, F32),
             pltpu.VMEM((1, rows), F32),
-            pltpu.SemaphoreType.DMA((8,)),
+            pltpu.SemaphoreType.DMA((11,)),
         ],
         compiler_params=params,
         name="pack_rows",
-    )(adjoint, kappa, box_row, cell_row, lattice_frac, dres_dx, dobj_dx)
+    )(
+        adjoint,
+        kappa,
+        box_row,
+        cell_row,
+        lattice_frac,
+        dres_dx,
+        dobj_dx,
+        conv,
+        jac_diag,
+        source,
+        face_scale,
+    )
     got = lax.all_to_all(packed, "blk", 0, 0, axis_index_groups=[spread(boxes)], tiled=True)
 
     pairs = [(i, i + 1) for i in range(boxes - 1)]
@@ -389,39 +405,33 @@
 
     inner, edge = pl.pallas_call(
         sweep_kernel,
-        out_shape=(shape(*adjoint.shape), shape(2, 2 * fields + 2, *plane)),
-        in_specs=[hbm] * 6 + [pl.BlockSpec(memory_space=pl.ANY)],
+        out_shape=(
+            shape(*adjoint.shape),
+            shape(2 * (2 * fields + 2) + fields * fields, *plane),
+        ),
+        in_specs=[vmem] * 6,
         out_specs=(hbm, vmem),
         scratch_shapes=[
             pltpu.VMEM(adjoint.shape, F32),
-            pltpu.VMEM(jac_diag.shape, F32),
-            pltpu.SMEM(conv.shape, F32),
-            pltpu.VMEM(face_scale.shape, F32),
-            pltpu.VMEM(kappa.shape, F32),
-            pltpu.VMEM(source.shape, F32),
-            pltpu.VMEM(adjoint.shape, F32),
-            pltpu.SemaphoreType.DMA((15,)),
             pltpu.SemaphoreType.DMA((4,)),
         ],
         compiler_params=params,
         name="sweep_planes",
-    )(adjoint, jac_diag, conv, face_scale, kappa, source, to_mate)
+    )(adj, jac, fill, face, kap, src)
 
     box_sens, residual = pl.pallas_call(
         sum_kernel,
         out_shape=(shape(3, LAT**3), shape(*adjoint.shape)),
-        in_specs=[vmem] * 4 + [hbm, hbm],
+        in_specs=[vmem] * 4 + [hbm],
         out_specs=(vmem, hbm),
         scratch_shapes=[
-            pltpu.SMEM(conv.shape, F32),
             pltpu.VMEM((2, fields) + plane, F32),
-            pltpu.SemaphoreType.DMA,
             pltpu.SemaphoreType.DMA((2,)),
         ],
-        input_output_aliases={5: 1},
+        input_output_aliases={4: 1},
         compiler_params=params,
         name="sum_rows",
-    )(got, edge, mate, other, conv, inner)
+    )(got, edge, mate, other, inner)
     return residual, box_sens
 
 

time: 21.6 us -> 19.9 us (0.921)
  waiting for transfers between devices: 0.01 us -> 3.55 us
  starting transfers between devices: 11.4 us -> 8.67 us
  Pallas kernels: 9.13 us -> 6.71 us
    all_to_all x1, waiting for transfers between devices: 0.01 us -> 3.54 us  [local(): lax.all_to_all(packed, 'blk', 0, 0, axis_index_groups=[spread(boxes)], ti...]
    ppermute x1, starting transfers between devices: 2.92 us -> 0.15 us  [local(): mate = lax.ppermute(to_mate, 'blk', both_ways[0])]
    pallas_call x1, Pallas kernels: 2.99 us -> 1.52 us  [local(): pl.pallas_call(sweep_kernel, out_shape=(shape(*adjoint.shape), shape(2 *...]
    pallas_call x1, Pallas kernels: 3.8 us -> 2.64 us  [local(): pl.pallas_call(sum_kernel, out_shape=(shape(3, LAT ** 3), shape(*adjoint....]
  transfers between devices with their start and end apart: 3 -> 3, of which waited for: 0 -> 1; matrix products, arithmetic and copies ran while one was open for 0% -> 0% of each run, Pallas kernels for 14% -> 8%
where the time goes in v4:
time: 19.9 us; the launch traced here: 19.6 us
  starting transfers between devices  8.67 us (44%)
  Pallas kernels  6.71 us (34%)
  waiting for transfers between devices  3.55 us (18%)
  between operations  0.68 us (3%)
    all_to_all x1, starting transfers between devices, local(): lax.all_to_all(packed, 'blk', 0, 0, axis_index_groups=[spread(boxes)], ti...  7.87 us
    all_to_all x1, waiting for transfers between devices, local(): lax.all_to_all(packed, 'blk', 0, 0, axis_index_groups=[spread(boxes)], ti...  3.54 us
    pallas_call x1, Pallas kernels, local(): pl.pallas_call(sum_kernel, out_shape=(shape(3, LAT ** 3), shape(*adjoint....  2.64 us
    pallas_call x1, Pallas kernels, local(): pl.pallas_call(functools.partial(pack_kernel, boxes, cap), out_shape=(sha...  2.55 us
    pallas_call x1, Pallas kernels, local(): pl.pallas_call(sweep_kernel, out_shape=(shape(*adjoint.shape), shape(2 *...  1.52 us
    ppermute x1, starting transfers between devices, local(): other = lax.ppermute(to_other, 'blk', both_ways[1])  0.65 us
  transfers between devices with their start and end apart: 3, of which 1 were waited for; matrix products, arithmetic and copies ran while one was open for 0% of the time, Pallas kernels for 8%

profile of v4, /device:TPU:0, one launch (start us, length us, event | category | flops | bytes accessed | tf_op | source)
XLA Modules:
  0.0 19.6 jit_solution(8985888888416647482)
XLA Ops:
  0.6 2.6 %pack_rows.1 = (f32[16,7,2,128]{3,2,1,0:T(2,128)}, f32[6,8,128]{2,1,0:T(8,128)S(1)}, f32[6,8,128]{2,1,0:T(8,128)S(1)}, f32[5,16,8,128]{3,2,1,0:T(8,128)S(1)}, f3...) custom-call(f32[5,16,8,128]{3,2,1,0:T(8,128)} %adj_hbm.1, ...), custom_call_target="tpu_custom_call" | custom-call | tf_op jit(solution)/shard_map/pack_rows/pallas_call | solution.py:359
  3.2 7.9 %all-to-all-start = ((f32[16,7,2,128]{3,2,1,0:T(2,128)}), f32[16,7,2,128]{3,2,1,0:T(2,128)S(1)}, u32[]{:S(2)}, u32[]{:S(2)}) async-start(f32[16,7,2,128]{3,2,1,0:T(2,128)} %get-tuple-element.15), calls=%async_computation | async-start | bytes 229376 | tf_op jit(solution)/shard_map/all_to_all | solution.py:399
  11.1 0.1 collective-permute-start
  11.2 0.7 %collective-permute-start.1 = (f32[6,8,128]{2,1,0:T(8,128)S(1)}, f32[6,8,128]{2,1,0:T(8,128)S(1)}, u32[]{:S(2)}, u32[]{:S(2)}) collective-permute-start(f32[6,8,128]{2,1,0:T(8,128)S(1)} %get-tuple-element.24), channel_id=1, source_target_pairs={{1,2},{2,1},{3,4},{4,3},{5,6},{6,5},{7,8},{8,7},{9,10},{10,9},{11,... | collective-permute-start | bytes 73736 | tf_op jit(solution)/shard_map/ppermute | solution.py:404
  11.9 1.5 %sweep_planes.1 = (f32[5,16,8,128]{3,2,1,0:T(8,128)}, f32[49,8,128]{2,1,0:T(8,128)S(1)}) custom-call(f32[5,16,8,128]{3,2,1,0:T(8,128)S(1)} %get-tuple-element.16.adj_ref, f32[5,5,16,8,128]{4,3,2,1,0:T(8,128)S(1)} %get-tuple-element.17.jac_ref, f32[5,3,5,8,128]{4,3,2,1,0:T(8,128)S(1)} %get-tuple-element.18.fill_ref, ...), custom_call_target="tpu_custom_call" | custom-call | tf_op jit(solution)/shard_map/sweep_planes/pallas_call | solution.py:406
  13.4 0.0 collective-permute-done.mate_ref
  13.4 0.0 collective-permute-done.1.other_ref
  13.4 3.5 %all-to-all-done.got_ref = f32[16,7,2,128]{3,2,1,0:T(2,128)S(1)} async-done(((f32[16,7,2,128]{3,2,1,0:T(2,128)}), f32[16,7,2,128]{3,2,1,0:T(2,128)S(1)}, u32[]{:S(2)}, u32[]{:S(2)}) %all-to-all-start) | async-done | bytes 114720 | tf_op jit(solution)/shard_map/all_to_all | solution.py:399
  17.0 2.6 %sum_rows.1 = (f32[3,4096]{1,0:T(4,128)}, f32[5,16,8,128]{3,2,1,0:T(8,128)}) custom-call(f32[16,7,2,128]{3,2,1,0:T(2,128)S(1)} %all-to-all-done.got_ref, f32[49,8,128]{2,1,0:T(8,128)S(1)} %get-tuple-element.22.edge_ref, f32[6,8,128]{2,1,0:T(8,128)S(1)} %collective-permute-done.mate_ref, ...), custom_call_target="tpu_custom_call", output_to_operand_aliasing={{1}: (4, {})} | custom-call | tf_op jit(solution)/shard_map/sum_rows/pallas_call | solution.py:422
Async XLA Ops:
  3.2 13.8 %all-to-all-start = ((f32[16,7,2,128]{3,2,1,0:T(2,128)}), f32[16,7,2,128]{3,2,1,0:T(2,128)S(1)}, u32[]{:S(2)}, u32[]{:S(2)}) async-start(f32[16,7,2,128]{3,2,1,0:T(2,128)} %get-tuple-element.15), calls=%async_computation | async-start | bytes 229376 | tf_op jit(solution)/shard_map/all_to_all | solution.py:399
  11.1 2.3 %collective-permute-start = (f32[6,8,128]{2,1,0:T(8,128)S(1)}, f32[6,8,128]{2,1,0:T(8,128)S(1)}, u32[]{:S(2)}, u32[]{:S(2)}) collective-permute-start(f32[6,8,128]{2,1,0:T(8,128)S(1)} %get-tuple-element.23), channel_id=1, source_target_pairs={{0,1},{1,0},{2,3},{3,2},{4,5},{5,4},{6,7},{7,6},{8,9},{9,8},{10,11... | collective-permute-start | bytes 73736 | tf_op jit(solution)/shard_map/ppermute | solution.py:403
  11.2 2.2 %collective-permute-start.1 = (f32[6,8,128]{2,1,0:T(8,128)S(1)}, f32[6,8,128]{2,1,0:T(8,128)S(1)}, u32[]{:S(2)}, u32[]{:S(2)}) collective-permute-start(f32[6,8,128]{2,1,0:T(8,128)S(1)} %get-tuple-element.24), channel_id=1, source_target_pairs={{1,2},{2,1},{3,4},{4,3},{5,6},{6,5},{7,8},{8,7},{9,10},{10,9},{11,... | collective-permute-start | bytes 73736 | tf_op jit(solution)/shard_map/ppermute | solution.py:404

commit v5 on v4

--- a/solution.py
+++ b/solution.py
@@ -10,6 +10,7 @@
 LAT = 16
 CHUNK = 256
 ROW = 7
+GROUP = 4
 SMALL = 12 * 2**20
 F32 = jnp.float32
 BF16 = jnp.bfloat16
@@ -128,6 +129,7 @@
     total = jnp.zeros((boxes * 16, cap), F32)
     slots = lax.broadcasted_iota(jnp.int32, (cap, CHUNK), 0).astype(F32)
     per = CHUNK // lanes
+    lefts, rights = [], []
     for j in range(chunks):
         part = slice(j * CHUNK, (j + 1) * CHUNK)
         acc = dobj_ref[:, part]
@@ -142,11 +144,18 @@
         hi = values.astype(BF16).astype(F32)
         both = jnp.concatenate([hi, values - hi], 0)
         mine = box[:, part]
-        lhs = jnp.concatenate(
-            [jnp.where(mine == b, both, 0.0) for b in spread(boxes)], 0
-        ).astype(BF16)
-        rhs = (slots == ranks_ref[:, part]).astype(F32).astype(BF16)
-        total = total + lax.dot_general(lhs, rhs, NT, preferred_element_type=F32)
+        lefts.append(
+            jnp.concatenate([jnp.where(mine == b, both, 0.0) for b in spread(boxes)], 0).astype(BF16)
+        )
+        rights.append((slots == ranks_ref[:, part]).astype(F32).astype(BF16))
+        if len(lefts) == GROUP:
+            total = total + lax.dot_general(
+                jnp.concatenate(lefts, 1),
+                jnp.concatenate(rights, 1),
+                NT,
+                preferred_element_type=F32,
+            )
+            lefts, rights = [], []
     width = out_ref.shape[-1]
     for b in range(boxes):
         block = total[b * 16:b * 16 + ROW] + total[b * 16 + 8:b * 16 + 8 + ROW]
@@ -291,9 +300,9 @@
     inner = LAT - 1
     points = lax.broadcasted_iota(jnp.int32, (LAT, cap), 0).astype(F32)
     both = jnp.zeros((6 * LAT, LAT * LAT), F32)
+    sent = edges()
+    lefts, rights_hi, rights_lo = [], [], []
     for s in range(sources):
-        if s == sources // 4:
-            sent = edges()
         block = jnp.concatenate([got_ref[s, :, i, :] for i in range(cuts)], 1)
         cell = block[6:7]
         first = jnp.floor((cell + 0.5) * (1.0 / (inner * inner)))
@@ -308,11 +317,17 @@
             )
         left = jnp.concatenate([tent[0] * block[c:c + 1] for c in range(3)], 0)
         right = jnp.concatenate([tent[1][b:b + 1] * tent[2] for b in range(LAT)], 0)
-        left_hi, left_lo = split_two(left)
+        lefts.append(jnp.concatenate(split_two(left), 0))
         right_hi, right_lo = split_two(right)
-        lhs = jnp.concatenate([left_hi, left_lo], 0)
-        both = both + lax.dot_general(lhs, right_hi, NT, preferred_element_type=F32)
-        both = both + lax.dot_general(lhs, right_lo, NT, preferred_element_type=F32)
+        rights_hi.append(right_hi)
+        rights_lo.append(right_lo)
+        if len(lefts) == GROUP:
+            lhs = jnp.concatenate(lefts, 1)
+            for rights in (rights_hi, rights_lo):
+                both = both + lax.dot_general(
+                    lhs, jnp.concatenate(rights, 1), NT, preferred_element_type=F32
+                )
+            lefts, rights_hi, rights_lo = [], [], []
     result = both[:3 * LAT] + both[3 * LAT:]
     for c in range(3):
         for a in range(LAT):
@@ -359,7 +374,7 @@
     packed, to_mate, to_other, adj, kap, fill, jac, src, face = pl.pallas_call(
         functools.partial(pack_kernel, boxes, cap),
         out_shape=(
-            shape(*payload),
+            pltpu.VMEM(payload, F32),
             halo,
             halo,
             shape(*adjoint.shape),

time: 19.9 us -> 20 us (level)
  no operation moved by 1% of the time
where the time goes in v5:
time: 20 us; the launch traced here: 19.7 us
  starting transfers between devices  8.67 us (43%)
  Pallas kernels  6.82 us (34%)
  waiting for transfers between devices  3.55 us (18%)
  between operations  0.68 us (3%)
    all_to_all x1, starting transfers between devices, local(): lax.all_to_all(packed, 'blk', 0, 0, axis_index_groups=[spread(boxes)], ti...  7.87 us
    all_to_all x1, waiting for transfers between devices, local(): lax.all_to_all(packed, 'blk', 0, 0, axis_index_groups=[spread(boxes)], ti...  3.54 us
    pallas_call x1, Pallas kernels, local(): pl.pallas_call(sum_kernel, out_shape=(shape(3, LAT ** 3), shape(*adjoint....  2.75 us
    pallas_call x1, Pallas kernels, local(): pl.pallas_call(functools.partial(pack_kernel, boxes, cap), out_shape=(plt...  2.55 us
    pallas_call x1, Pallas kernels, local(): pl.pallas_call(sweep_kernel, out_shape=(shape(*adjoint.shape), shape(2 *...  1.52 us
    ppermute x1, starting transfers between devices, local(): other = lax.ppermute(to_other, 'blk', both_ways[1])  0.65 us
  transfers between devices with their start and end apart: 3, of which 1 were waited for; matrix products, arithmetic and copies ran while one was open for 0% of the time, Pallas kernels for 8%

profile of v5, /device:TPU:0, one launch (start us, length us, event | category | flops | bytes accessed | tf_op | source)
XLA Modules:
  0.0 19.7 jit_solution(11258231132462306744)
XLA Ops:
  0.6 2.6 %pack_rows.1 = (f32[16,7,2,128]{3,2,1,0:T(2,128)}, f32[6,8,128]{2,1,0:T(8,128)S(1)}, f32[6,8,128]{2,1,0:T(8,128)S(1)}, f32[5,16,8,128]{3,2,1,0:T(8,128)S(1)}, f3...) custom-call(f32[5,16,8,128]{3,2,1,0:T(8,128)} %adj_hbm.1, ...), custom_call_target="tpu_custom_call" | custom-call | tf_op jit(solution)/shard_map/pack_rows/pallas_call | solution.py:374
  3.2 7.9 %all-to-all-start = ((f32[16,7,2,128]{3,2,1,0:T(2,128)}), f32[16,7,2,128]{3,2,1,0:T(2,128)S(1)}, u32[]{:S(2)}, u32[]{:S(2)}) async-start(f32[16,7,2,128]{3,2,1,0:T(2,128)} %get-tuple-element.15), calls=%async_computation | async-start | bytes 229376 | tf_op jit(solution)/shard_map/all_to_all | solution.py:414
  11.1 0.1 collective-permute-start
  11.2 0.7 %collective-permute-start.1 = (f32[6,8,128]{2,1,0:T(8,128)S(1)}, f32[6,8,128]{2,1,0:T(8,128)S(1)}, u32[]{:S(2)}, u32[]{:S(2)}) collective-permute-start(f32[6,8,128]{2,1,0:T(8,128)S(1)} %get-tuple-element.24), channel_id=1, source_target_pairs={{1,2},{2,1},{3,4},{4,3},{5,6},{6,5},{7,8},{8,7},{9,10},{10,9},{11,... | collective-permute-start | bytes 73736 | tf_op jit(solution)/shard_map/ppermute | solution.py:419
  11.9 1.5 %sweep_planes.1 = (f32[5,16,8,128]{3,2,1,0:T(8,128)}, f32[49,8,128]{2,1,0:T(8,128)S(1)}) custom-call(f32[5,16,8,128]{3,2,1,0:T(8,128)S(1)} %get-tuple-element.16.adj_ref, f32[5,5,16,8,128]{4,3,2,1,0:T(8,128)S(1)} %get-tuple-element.17.jac_ref, f32[5,3,5,8,128]{4,3,2,1,0:T(8,128)S(1)} %get-tuple-element.18.fill_ref, ...), custom_call_target="tpu_custom_call" | custom-call | tf_op jit(solution)/shard_map/sweep_planes/pallas_call | solution.py:421
  13.4 0.0 collective-permute-done.mate_ref
  13.4 0.0 collective-permute-done.1.other_ref
  13.4 3.5 %all-to-all-done.got_ref = f32[16,7,2,128]{3,2,1,0:T(2,128)S(1)} async-done(((f32[16,7,2,128]{3,2,1,0:T(2,128)}), f32[16,7,2,128]{3,2,1,0:T(2,128)S(1)}, u32[]{:S(2)}, u32[]{:S(2)}) %all-to-all-start) | async-done | bytes 114720 | tf_op jit(solution)/shard_map/all_to_all | solution.py:414
  17.0 2.7 %sum_rows.1 = (f32[3,4096]{1,0:T(4,128)}, f32[5,16,8,128]{3,2,1,0:T(8,128)}) custom-call(f32[16,7,2,128]{3,2,1,0:T(2,128)S(1)} %all-to-all-done.got_ref, f32[49,8,128]{2,1,0:T(8,128)S(1)} %get-tuple-element.22.edge_ref, f32[6,8,128]{2,1,0:T(8,128)S(1)} %collective-permute-done.mate_ref, ...), custom_call_target="tpu_custom_call", output_to_operand_aliasing={{1}: (4, {})} | custom-call | tf_op jit(solution)/shard_map/sum_rows/pallas_call | solution.py:437
Async XLA Ops:
  3.2 13.8 %all-to-all-start = ((f32[16,7,2,128]{3,2,1,0:T(2,128)}), f32[16,7,2,128]{3,2,1,0:T(2,128)S(1)}, u32[]{:S(2)}, u32[]{:S(2)}) async-start(f32[16,7,2,128]{3,2,1,0:T(2,128)} %get-tuple-element.15), calls=%async_computation | async-start | bytes 229376 | tf_op jit(solution)/shard_map/all_to_all | solution.py:414
  11.1 2.3 %collective-permute-start = (f32[6,8,128]{2,1,0:T(8,128)S(1)}, f32[6,8,128]{2,1,0:T(8,128)S(1)}, u32[]{:S(2)}, u32[]{:S(2)}) collective-permute-start(f32[6,8,128]{2,1,0:T(8,128)S(1)} %get-tuple-element.23), channel_id=1, source_target_pairs={{0,1},{1,0},{2,3},{3,2},{4,5},{5,4},{6,7},{7,6},{8,9},{9,8},{10,11... | collective-permute-start | bytes 73736 | tf_op jit(solution)/shard_map/ppermute | solution.py:418
  11.2 2.2 %collective-permute-start.1 = (f32[6,8,128]{2,1,0:T(8,128)S(1)}, f32[6,8,128]{2,1,0:T(8,128)S(1)}, u32[]{:S(2)}, u32[]{:S(2)}) collective-permute-start(f32[6,8,128]{2,1,0:T(8,128)S(1)} %get-tuple-element.24), channel_id=1, source_target_pairs={{1,2},{2,1},{3,4},{4,3},{5,6},{6,5},{7,8},{8,7},{9,10},{10,9},{11,... | collective-permute-start | bytes 73736 | tf_op jit(solution)/shard_map/ppermute | solution.py:419

commit v6 on v4

--- a/solution.py
+++ b/solution.py
@@ -36,9 +36,9 @@
     order = []
     for k in range(quarter):
         order += [
-            quarter + k,
+            k,
             3 * quarter + (k + 2) % quarter,
-            (k + 3) % quarter,
+            quarter + (k + 3) % quarter,
             2 * quarter + (k + 1) % quarter,
         ]
     return order

time: 19.9 us -> 21.1 us (1.060)
  waiting for transfers between devices: 3.55 us -> 4.98 us
    all_to_all x1, waiting for transfers between devices: 3.54 us -> 4.97 us  [local(): lax.all_to_all(packed, 'blk', 0, 0, axis_index_groups=[spread(boxes)], ti...]
    all_to_all x1, starting transfers between devices: 7.87 us -> 7.4 us  [local(): lax.all_to_all(packed, 'blk', 0, 0, axis_index_groups=[spread(boxes)], ti...]
    ppermute x1, starting transfers between devices: 0.15 us -> 0.41 us  [local(): mate = lax.ppermute(to_mate, 'blk', both_ways[0])]
  transfers between devices with their start and end apart: 3 -> 3, of which waited for: 1 -> 1; matrix products, arithmetic and copies ran while one was open for 0% -> 0% of each run, Pallas kernels for 8% -> 7%
where the time goes in v6:
time: 21.1 us; the launch traced here: 20.8 us
  starting transfers between devices  8.46 us (40%)
  Pallas kernels  6.71 us (32%)
  waiting for transfers between devices  4.98 us (24%)
  between operations  0.68 us (3%)
    all_to_all x1, starting transfers between devices, local(): lax.all_to_all(packed, 'blk', 0, 0, axis_index_groups=[spread(boxes)], ti...  7.4 us
    all_to_all x1, waiting for transfers between devices, local(): lax.all_to_all(packed, 'blk', 0, 0, axis_index_groups=[spread(boxes)], ti...  4.97 us
    pallas_call x1, Pallas kernels, local(): pl.pallas_call(sum_kernel, out_shape=(shape(3, LAT ** 3), shape(*adjoint....  2.64 us
    pallas_call x1, Pallas kernels, local(): pl.pallas_call(functools.partial(pack_kernel, boxes, cap), out_shape=(sha...  2.55 us
    pallas_call x1, Pallas kernels, local(): pl.pallas_call(sweep_kernel, out_shape=(shape(*adjoint.shape), shape(2 *...  1.52 us
    ppermute x1, starting transfers between devices, local(): other = lax.ppermute(to_other, 'blk', both_ways[1])  0.65 us
  transfers between devices with their start and end apart: 3, of which 1 were waited for; matrix products, arithmetic and copies ran while one was open for 0% of the time, Pallas kernels for 7%

profile of v6, /device:TPU:0, one launch (start us, length us, event | category | flops | bytes accessed | tf_op | source)
XLA Modules:
  0.0 20.8 jit_solution(4456575968920876552)
XLA Ops:
  0.6 2.6 %pack_rows.1 = (f32[16,7,2,128]{3,2,1,0:T(2,128)}, f32[6,8,128]{2,1,0:T(8,128)S(1)}, f32[6,8,128]{2,1,0:T(8,128)S(1)}, f32[5,16,8,128]{3,2,1,0:T(8,128)S(1)}, f3...) custom-call(f32[5,16,8,128]{3,2,1,0:T(8,128)} %adj_hbm.1, ...), custom_call_target="tpu_custom_call" | custom-call | tf_op jit(solution)/shard_map/pack_rows/pallas_call | solution.py:359
  3.2 7.4 %all-to-all-start = ((f32[16,7,2,128]{3,2,1,0:T(2,128)}), f32[16,7,2,128]{3,2,1,0:T(2,128)S(1)}, u32[]{:S(2)}, u32[]{:S(2)}) async-start(f32[16,7,2,128]{3,2,1,0:T(2,128)} %get-tuple-element.15), calls=%async_computation | async-start | bytes 229376 | tf_op jit(solution)/shard_map/all_to_all | solution.py:399
  10.6 0.4 %collective-permute-start = (f32[6,8,128]{2,1,0:T(8,128)S(1)}, f32[6,8,128]{2,1,0:T(8,128)S(1)}, u32[]{:S(2)}, u32[]{:S(2)}) collective-permute-start(f32[6,8,128]{2,1,0:T(8,128)S(1)} %get-tuple-element.23), channel_id=1, source_target_pairs={{0,1},{1,0},{2,3},{3,2},{4,5},{5,4},{6,7},{7,6},{8,9},{9,8},{10,11... | collective-permute-start | bytes 73736 | tf_op jit(solution)/shard_map/ppermute | solution.py:403
  11.0 0.7 %collective-permute-start.1 = (f32[6,8,128]{2,1,0:T(8,128)S(1)}, f32[6,8,128]{2,1,0:T(8,128)S(1)}, u32[]{:S(2)}, u32[]{:S(2)}) collective-permute-start(f32[6,8,128]{2,1,0:T(8,128)S(1)} %get-tuple-element.24), channel_id=1, source_target_pairs={{1,2},{2,1},{3,4},{4,3},{5,6},{6,5},{7,8},{8,7},{9,10},{10,9},{11,... | collective-permute-start | bytes 73736 | tf_op jit(solution)/shard_map/ppermute | solution.py:404
  11.7 1.5 %sweep_planes.1 = (f32[5,16,8,128]{3,2,1,0:T(8,128)}, f32[49,8,128]{2,1,0:T(8,128)S(1)}) custom-call(f32[5,16,8,128]{3,2,1,0:T(8,128)S(1)} %get-tuple-element.16.adj_ref, f32[5,5,16,8,128]{4,3,2,1,0:T(8,128)S(1)} %get-tuple-element.17.jac_ref, f32[5,3,5,8,128]{4,3,2,1,0:T(8,128)S(1)} %get-tuple-element.18.fill_ref, ...), custom_call_target="tpu_custom_call" | custom-call | tf_op jit(solution)/shard_map/sweep_planes/pallas_call | solution.py:406
  13.2 0.0 collective-permute-done.mate_ref
  13.2 0.0 collective-permute-done.1.other_ref
  13.2 5.0 %all-to-all-done.got_ref = f32[16,7,2,128]{3,2,1,0:T(2,128)S(1)} async-done(((f32[16,7,2,128]{3,2,1,0:T(2,128)}), f32[16,7,2,128]{3,2,1,0:T(2,128)S(1)}, u32[]{:S(2)}, u32[]{:S(2)}) %all-to-all-start) | async-done | bytes 114720 | tf_op jit(solution)/shard_map/all_to_all | solution.py:399
  18.2 2.6 %sum_rows.1 = (f32[3,4096]{1,0:T(4,128)}, f32[5,16,8,128]{3,2,1,0:T(8,128)}) custom-call(f32[16,7,2,128]{3,2,1,0:T(2,128)S(1)} %all-to-all-done.got_ref, f32[49,8,128]{2,1,0:T(8,128)S(1)} %get-tuple-element.22.edge_ref, f32[6,8,128]{2,1,0:T(8,128)S(1)} %collective-permute-done.mate_ref, ...), custom_call_target="tpu_custom_call", output_to_operand_aliasing={{1}: (4, {})} | custom-call | tf_op jit(solution)/shard_map/sum_rows/pallas_call | solution.py:422
Async XLA Ops:
  3.2 15.0 %all-to-all-start = ((f32[16,7,2,128]{3,2,1,0:T(2,128)}), f32[16,7,2,128]{3,2,1,0:T(2,128)S(1)}, u32[]{:S(2)}, u32[]{:S(2)}) async-start(f32[16,7,2,128]{3,2,1,0:T(2,128)} %get-tuple-element.15), calls=%async_computation | async-start | bytes 229376 | tf_op jit(solution)/shard_map/all_to_all | solution.py:399
  10.6 2.6 %collective-permute-start = (f32[6,8,128]{2,1,0:T(8,128)S(1)}, f32[6,8,128]{2,1,0:T(8,128)S(1)}, u32[]{:S(2)}, u32[]{:S(2)}) collective-permute-start(f32[6,8,128]{2,1,0:T(8,128)S(1)} %get-tuple-element.23), channel_id=1, source_target_pairs={{0,1},{1,0},{2,3},{3,2},{4,5},{5,4},{6,7},{7,6},{8,9},{9,8},{10,11... | collective-permute-start | bytes 73736 | tf_op jit(solution)/shard_map/ppermute | solution.py:403
  11.0 2.2 %collective-permute-start.1 = (f32[6,8,128]{2,1,0:T(8,128)S(1)}, f32[6,8,128]{2,1,0:T(8,128)S(1)}, u32[]{:S(2)}, u32[]{:S(2)}) collective-permute-start(f32[6,8,128]{2,1,0:T(8,128)S(1)} %get-tuple-element.24), channel_id=1, source_target_pairs={{1,2},{2,1},{3,4},{4,3},{5,6},{6,5},{7,8},{8,7},{9,10},{10,9},{11,... | collective-permute-start | bytes 73736 | tf_op jit(solution)/shard_map/ppermute | solution.py:404

commit v7 on v6

--- a/solution.py
+++ b/solution.py
@@ -36,10 +36,10 @@
     order = []
     for k in range(quarter):
         order += [
-            k,
-            3 * quarter + (k + 2) % quarter,
-            quarter + (k + 3) % quarter,
-            2 * quarter + (k + 1) % quarter,
+            count - 1 - k,
+            (k + 2) % quarter,
+            2 * quarter + (k + 3) % quarter,
+            quarter + (k + 1) % quarter,
         ]
     return order
 
@@ -249,51 +249,37 @@
     wait_all(sent)
 
 
-def sum_kernel(
-    got_ref,
-    edge_ref,
-    mate_ref,
-    other_ref,
-    part_hbm,
-    out_ref,
-    res_hbm,
-    res_ref,
-    out_sems,
-):
-    del part_hbm
+def edge_kernel(edge_ref, mate_ref, other_ref, after_ref, part_hbm, res_hbm, res_ref, out_sems):
+    del after_ref, part_hbm
     fields, planes = res_hbm.shape[:2]
-
-    def edges():
-        even = on_even()
-        copies = []
-        for e in (0, 1):
-            beyond = [
-                jnp.where(even == (e == 0), other_ref[f], mate_ref[f]) for f in range(fields + 1)
-            ]
-            base = e * (2 * fields + 2)
-            kap = edge_ref[base + 2 * fields]
-            scale = edge_ref[base + 2 * fields + 1] * (0.5 if e else -0.5)
-            terms = [scale * beyond[k] for k in range(fields)]
-            weight = 0.5 * (kap + beyond[fields])
-            extra = 0.5 * beyond[fields]
-            for f in range(fields):
-                total = edge_ref[base + f] - weight * beyond[f] + extra * edge_ref[base + fields + f]
-                for k in range(fields):
-                    total = total + edge_ref[4 * fields + 4 + k * fields + f] * terms[k]
-                res_ref[e, f] = total
-            copies.append(
-                pltpu.make_async_copy(res_ref.at[e], res_hbm.at[:, e * (planes - 1)], out_sems.at[e])
-            )
-        return start_all(copies)
-
+    even = on_even()
+    copies = []
+    for e in (0, 1):
+        beyond = [jnp.where(even == (e == 0), other_ref[f], mate_ref[f]) for f in range(fields + 1)]
+        base = e * (2 * fields + 2)
+        kap = edge_ref[base + 2 * fields]
+        scale = edge_ref[base + 2 * fields + 1] * (0.5 if e else -0.5)
+        terms = [scale * beyond[k] for k in range(fields)]
+        weight = 0.5 * (kap + beyond[fields])
+        extra = 0.5 * beyond[fields]
+        for f in range(fields):
+            total = edge_ref[base + f] - weight * beyond[f] + extra * edge_ref[base + fields + f]
+            for k in range(fields):
+                total = total + edge_ref[4 * fields + 4 + k * fields + f] * terms[k]
+            res_ref[e, f] = total
+        copy = pltpu.make_async_copy(res_ref.at[e], res_hbm.at[:, e * (planes - 1)], out_sems.at[e])
+        copy.start()
+        copies.append(copy)
+    wait_all(copies)
+
+
+def sum_kernel(got_ref, out_ref):
     sources, _, cuts, width = got_ref.shape
     cap = cuts * width
     inner = LAT - 1
     points = lax.broadcasted_iota(jnp.int32, (LAT, cap), 0).astype(F32)
     both = jnp.zeros((6 * LAT, LAT * LAT), F32)
     for s in range(sources):
-        if s == sources // 4:
-            sent = edges()
         block = jnp.concatenate([got_ref[s, :, i, :] for i in range(cuts)], 1)
         cell = block[6:7]
         first = jnp.floor((cell + 0.5) * (1.0 / (inner * inner)))
@@ -317,7 +303,6 @@
     for c in range(3):
         for a in range(LAT):
             out_ref[c:c + 1, a * LAT * LAT:(a + 1) * LAT * LAT] = result[c * LAT + a:c * LAT + a + 1]
-    wait_all(sent)
 
 
 def local(
@@ -419,19 +404,28 @@
         name="sweep_planes",
     )(adj, jac, fill, face, kap, src)
 
-    box_sens, residual = pl.pallas_call(
+    box_sens = pl.pallas_call(
         sum_kernel,
-        out_shape=(shape(3, LAT**3), shape(*adjoint.shape)),
-        in_specs=[vmem] * 4 + [hbm],
-        out_specs=(vmem, hbm),
+        out_shape=shape(3, LAT**3),
+        in_specs=[vmem],
+        out_specs=vmem,
+        compiler_params=params,
+        name="sum_rows",
+    )(got)
+
+    residual = pl.pallas_call(
+        edge_kernel,
+        out_shape=shape(*adjoint.shape),
+        in_specs=[vmem] * 3 + [pl.BlockSpec(memory_space=pl.ANY), hbm],
+        out_specs=hbm,
         scratch_shapes=[
             pltpu.VMEM((2, fields) + plane, F32),
             pltpu.SemaphoreType.DMA((2,)),
         ],
-        input_output_aliases={4: 1},
+        input_output_aliases={4: 0},
         compiler_params=params,
-        name="sum_rows",
-    )(got, edge, mate, other, inner)
+        name="edge_planes",
+    )(edge, mate, other, box_sens, inner)
     return residual, box_sens
 
 

time: 21.1 us -> 19.9 us (0.943)
  waiting for transfers between devices: 4.98 us -> 1.65 us
  starting transfers between devices: 8.46 us -> 9.61 us
  local copies, waits for them, and re-layouts: 0 us -> 0.84 us
    all_to_all x1, waiting for transfers between devices: 4.97 us -> 1.64 us  [local(): lax.all_to_all(packed, 'blk', 0, 0, axis_index_groups=[spread(boxes)], ti...]
    all_to_all x1, starting transfers between devices: 7.4 us -> 8.81 us  [local(): lax.all_to_all(packed, 'blk', 0, 0, axis_index_groups=[spread(boxes)], ti...]
    unnamed x0 -> x2, local copies, waits for them, and re-layouts: none -> 0.84 us
    ppermute x1, starting transfers between devices: 0.41 us -> 0.16 us  [local(): mate = lax.ppermute(to_mate, 'blk', both_ways[0])]
    pallas_call x1 -> x2, Pallas kernels: 2.64 us -> 2.77 us  [the longest x1 2.11 us: local(): pl.pallas_call(sum_kernel, out_shape=shape(3, LAT ** 3), in_specs=[vmem],...]
  transfers between devices with their start and end apart: 3 -> 3, of which waited for: 1 -> 1; matrix products, arithmetic and copies ran while one was open for 0% -> 0% of each run, Pallas kernels for 7% -> 19%
where the time goes in v7:
time: 19.9 us; the launch traced here: 19.6 us
  starting transfers between devices  9.61 us (48%)
  Pallas kernels  6.85 us (34%)
  waiting for transfers between devices  1.65 us (8%)
  local copies, waits for them, and re-layouts  0.84 us (4%)
  between operations  0.66 us (3%)
    all_to_all x1, starting transfers between devices, local(): lax.all_to_all(packed, 'blk', 0, 0, axis_index_groups=[spread(boxes)], ti...  8.81 us
    pallas_call x1, Pallas kernels, local(): pl.pallas_call(functools.partial(pack_kernel, boxes, cap), out_shape=(sha...  2.55 us
    pallas_call x1, Pallas kernels, local(): pl.pallas_call(sum_kernel, out_shape=shape(3, LAT ** 3), in_specs=[vmem],...  2.11 us
    all_to_all x1, waiting for transfers between devices, local(): lax.all_to_all(packed, 'blk', 0, 0, axis_index_groups=[spread(boxes)], ti...  1.64 us
    pallas_call x1, Pallas kernels, local(): pl.pallas_call(sweep_kernel, out_shape=(shape(*adjoint.shape), shape(2 *...  1.52 us
    unnamed x2, local copies, waits for them, and re-layouts  0.84 us
    pallas_call x1, Pallas kernels, local(): pl.pallas_call(edge_kernel, out_shape=shape(*adjoint.shape), in_specs=[vm...  0.66 us
    ppermute x1, starting transfers between devices, local(): other = lax.ppermute(to_other, 'blk', both_ways[1])  0.65 us
  transfers between devices with their start and end apart: 3, of which 1 were waited for; matrix products, arithmetic and copies ran while one was open for 0% of the time, Pallas kernels for 19%

profile of v7, /device:TPU:0, one launch (start us, length us, event | category | flops | bytes accessed | tf_op | source)
XLA Modules:
  0.0 19.6 jit_solution(15633872066245514940)
XLA Ops:
  0.6 2.6 %pack_rows.1 = (f32[16,7,2,128]{3,2,1,0:T(2,128)}, f32[6,8,128]{2,1,0:T(8,128)S(1)}, f32[6,8,128]{2,1,0:T(8,128)S(1)}, f32[5,16,8,128]{3,2,1,0:T(8,128)S(1)}, f3...) custom-call(f32[5,16,8,128]{3,2,1,0:T(8,128)} %adj_hbm.1, ...), custom_call_target="tpu_custom_call" | custom-call | tf_op jit(solution)/shard_map/pack_rows/pallas_call | solution.py:344
  3.2 8.8 %all-to-all-start = ((f32[16,7,2,128]{3,2,1,0:T(2,128)}), f32[16,7,2,128]{3,2,1,0:T(2,128)S(1)}, u32[]{:S(2)}, u32[]{:S(2)}) async-start(f32[16,7,2,128]{3,2,1,0:T(2,128)} %get-tuple-element.22), calls=%async_computation | async-start | bytes 229376 | tf_op jit(solution)/shard_map/all_to_all | solution.py:384
  12.0 0.2 collective-permute-start
  12.2 0.7 %collective-permute-start.1 = (f32[6,8,128]{2,1,0:T(8,128)S(1)}, f32[6,8,128]{2,1,0:T(8,128)S(1)}, u32[]{:S(2)}, u32[]{:S(2)}) collective-permute-start(f32[6,8,128]{2,1,0:T(8,128)S(1)} %get-tuple-element.21), channel_id=1, source_target_pairs={{1,2},{2,1},{3,4},{4,3},{5,6},{6,5},{7,8},{8,7},{9,10},{10,9},{11,... | collective-permute-start | bytes 73736 | tf_op jit(solution)/shard_map/ppermute | solution.py:389
  12.8 1.5 %sweep_planes.1 = (f32[5,16,8,128]{3,2,1,0:T(8,128)}, f32[49,8,128]{2,1,0:T(8,128)S(1)}) custom-call(f32[5,16,8,128]{3,2,1,0:T(8,128)S(1)} %get-tuple-element.13.adj_ref, f32[5,5,16,8,128]{4,3,2,1,0:T(8,128)S(1)} %get-tuple-element.14.jac_ref, f32[5,3,5,8,128]{4,3,2,1,0:T(8,128)S(1)} %get-tuple-element.15.fill_ref, ...), custom_call_target="tpu_custom_call" | custom-call | tf_op jit(solution)/shard_map/sweep_planes/pallas_call | solution.py:391
  14.3 1.6 %all-to-all-done.got_ref = f32[16,7,2,128]{3,2,1,0:T(2,128)S(1)} async-done(((f32[16,7,2,128]{3,2,1,0:T(2,128)}), f32[16,7,2,128]{3,2,1,0:T(2,128)S(1)}, u32[]{:S(2)}, u32[]{:S(2)}) %all-to-all-start) | async-done | bytes 114720 | tf_op jit(solution)/shard_map/all_to_all | solution.py:384
  16.0 2.1 %sum_rows.1.after_ref = f32[3,4096]{1,0:T(4,128)} custom-call(f32[16,7,2,128]{3,2,1,0:T(2,128)S(1)} %all-to-all-done.got_ref), custom_call_target="tpu_custom_call" | custom-call | tf_op jit(solution)/shard_map/sum_rows/pallas_call | solution.py:407
  18.1 0.0 collective-permute-done.mate_ref
  18.1 0.0 collective-permute-done.1.other_ref
  18.1 0.0 copy-start
  18.1 0.8 %copy-done = f32[3,4096]{1,0:T(4,128)S(1)} copy-done((f32[3,4096]{1,0:T(4,128)S(1)}, f32[3,4096]{1,0:T(4,128)}, u32[]{:S(2)}) %copy-start) | copy-done | bytes 49176
  18.9 0.7 %edge_planes.1 = f32[5,16,8,128]{3,2,1,0:T(8,128)} custom-call(f32[49,8,128]{2,1,0:T(8,128)S(1)} %get-tuple-element.19.edge_ref, f32[6,8,128]{2,1,0:T(8,128)S(1)} %collective-permute-done.mate_ref, f32[6,8,128]{2,1,0:T(8,128)S(1)} %collective-permute-done.1.other_ref, f32[3,4096]{1,0:T(4,128)S(1)} %copy-done, ...), custom_call_target="tpu_custom_call", output_to_operand_aliasing={{}: (4, {})} | custom-call | tf_op jit(solution)/shard_map/edge_planes/pallas_call | solution.py:416
Async XLA Ops:
  3.2 12.8 %all-to-all-start = ((f32[16,7,2,128]{3,2,1,0:T(2,128)}), f32[16,7,2,128]{3,2,1,0:T(2,128)S(1)}, u32[]{:S(2)}, u32[]{:S(2)}) async-start(f32[16,7,2,128]{3,2,1,0:T(2,128)} %get-tuple-element.22), calls=%async_computation | async-start | bytes 229376 | tf_op jit(solution)/shard_map/all_to_all | solution.py:384
  12.0 6.1 %collective-permute-start = (f32[6,8,128]{2,1,0:T(8,128)S(1)}, f32[6,8,128]{2,1,0:T(8,128)S(1)}, u32[]{:S(2)}, u32[]{:S(2)}) collective-permute-start(f32[6,8,128]{2,1,0:T(8,128)S(1)} %get-tuple-element.20), channel_id=1, source_target_pairs={{0,1},{1,0},{2,3},{3,2},{4,5},{5,4},{6,7},{7,6},{8,9},{9,8},{10,11... | collective-permute-start | bytes 73736 | tf_op jit(solution)/shard_map/ppermute | solution.py:388
  12.2 5.9 %collective-permute-start.1 = (f32[6,8,128]{2,1,0:T(8,128)S(1)}, f32[6,8,128]{2,1,0:T(8,128)S(1)}, u32[]{:S(2)}, u32[]{:S(2)}) collective-permute-start(f32[6,8,128]{2,1,0:T(8,128)S(1)} %get-tuple-element.21), channel_id=1, source_target_pairs={{1,2},{2,1},{3,4},{4,3},{5,6},{6,5},{7,8},{8,7},{9,10},{10,9},{11,... | collective-permute-start | bytes 73736 | tf_op jit(solution)/shard_map/ppermute | solution.py:389
  18.1 0.8 %copy-start = (f32[3,4096]{1,0:T(4,128)S(1)}, f32[3,4096]{1,0:T(4,128)}, u32[]{:S(2)}) copy-start(f32[3,4096]{1,0:T(4,128)} %sum_rows.1.after_ref) | copy-start | bytes 147460

commit v8 on v7

--- a/solution.py
+++ b/solution.py
@@ -69,7 +69,7 @@
     jac_hbm,
     src_hbm,
     face_hbm,
-    out_ref,
+    out_hbm,
     mate_ref,
     other_ref,
     adj_ref,
@@ -78,6 +78,7 @@
     jac_ref,
     src_ref,
     face_ref,
+    out_ref,
     conv_ref,
     box_ref,
     cell_ref,
@@ -86,6 +87,7 @@
     dobj_ref,
     ranks_ref,
     sems,
+    out_sem,
 ):
     fields, planes, _, lanes = adj_hbm.shape
     rows = planes * lanes
@@ -152,11 +154,14 @@
         block = total[b * 16:b * 16 + ROW] + total[b * 16 + 8:b * 16 + 8 + ROW]
         for i in range(cap // width):
             out_ref[b, :, i, :] = block[:, i * width:(i + 1) * width]
+    out_copy = pltpu.make_async_copy(out_ref, out_hbm, out_sem)
+    out_copy.start()
     wait_all(copies[7:])
     for k in range(fields):
         for d in range(3):
             for f in range(fields):
                 fill_ref[k, d, f] = jnp.full(kap_ref.shape[1:], conv_ref[k, d, f], F32)
+    out_copy.wait()
 
 
 def plane_residual(psi, kap, below, above, jac, face, src, conv):
@@ -355,8 +360,9 @@
             shape(*face_scale.shape),
         ),
         in_specs=[hbm] * 11,
-        out_specs=(vmem,) * 9,
+        out_specs=(hbm,) + (vmem,) * 8,
         scratch_shapes=[
+            pltpu.VMEM(payload, F32),
             pltpu.SMEM(conv.shape, F32),
             pltpu.VMEM((1, rows), jnp.int32),
             pltpu.VMEM((1, rows), jnp.int32),
@@ -365,6 +371,7 @@
             pltpu.VMEM(dobj_dx.shape, F32),
             pltpu.VMEM((1, rows), F32),
             pltpu.SemaphoreType.DMA((11,)),
+            pltpu.SemaphoreType.DMA,
         ],
         compiler_params=params,
         name="pack_rows",
@@ -416,7 +423,7 @@
     residual = pl.pallas_call(
         edge_kernel,
         out_shape=shape(*adjoint.shape),
-        in_specs=[vmem] * 3 + [pl.BlockSpec(memory_space=pl.ANY), hbm],
+        in_specs=[vmem] * 3 + [hbm, hbm],
         out_specs=hbm,
         scratch_shapes=[
             pltpu.VMEM((2, fields) + plane, F32),
@@ -425,7 +432,7 @@
         input_output_aliases={4: 0},
         compiler_params=params,
         name="edge_planes",
-    )(edge, mate, other, box_sens, inner)
+    )(edge, mate, other, *stay(box_sens), inner)
     return residual, box_sens
 
 

time: 19.9 us -> 18.9 us (0.950)
  local copies, waits for them, and re-layouts: 0.84 us -> 0 us
    unnamed x2 -> x0, local copies, waits for them, and re-layouts: 0.84 us -> none
  transfers between devices with their start and end apart: 3 -> 3, of which waited for: 1 -> 1; matrix products, arithmetic and copies ran while one was open for 0% -> 0% of each run, Pallas kernels for 19% -> 20%
where the time goes in v8:
time: 18.9 us; the launch traced here: 18.6 us
  starting transfers between devices  9.61 us (51%)
  Pallas kernels  6.68 us (35%)
  waiting for transfers between devices  1.65 us (9%)
  between operations  0.66 us (3%)
    all_to_all x1, starting transfers between devices, local(): lax.all_to_all(packed, 'blk', 0, 0, axis_index_groups=[spread(boxes)], ti...  8.81 us
    pallas_call x1, Pallas kernels, local(): pl.pallas_call(functools.partial(pack_kernel, boxes, cap), out_shape=(sha...  2.38 us
    pallas_call x1, Pallas kernels, local(): pl.pallas_call(sum_kernel, out_shape=shape(3, LAT ** 3), in_specs=[vmem],...  2.12 us
    all_to_all x1, waiting for transfers between devices, local(): lax.all_to_all(packed, 'blk', 0, 0, axis_index_groups=[spread(boxes)], ti...  1.64 us
    pallas_call x1, Pallas kernels, local(): pl.pallas_call(sweep_kernel, out_shape=(shape(*adjoint.shape), shape(2 *...  1.52 us
    pallas_call x1, Pallas kernels, local(): pl.pallas_call(edge_kernel, out_shape=shape(*adjoint.shape), in_specs=[vm...  0.66 us
    ppermute x1, starting transfers between devices, local(): other = lax.ppermute(to_other, 'blk', both_ways[1])  0.65 us
  transfers between devices with their start and end apart: 3, of which 1 were waited for; matrix products, arithmetic and copies ran while one was open for 0% of the time, Pallas kernels for 20%

profile of v8, /device:TPU:0, one launch (start us, length us, event | category | flops | bytes accessed | tf_op | source)
XLA Modules:
  0.0 18.6 jit_solution(8316246970260267935)
XLA Ops:
  0.6 2.4 %pack_rows.1 = (f32[16,7,2,128]{3,2,1,0:T(2,128)}, f32[6,8,128]{2,1,0:T(8,128)S(1)}, f32[6,8,128]{2,1,0:T(8,128)S(1)}, f32[5,16,8,128]{3,2,1,0:T(8,128)S(1)}, f3...) custom-call(f32[5,16,8,128]{3,2,1,0:T(8,128)} %adj_hbm.1, ...), custom_call_target="tpu_custom_call" | custom-call | tf_op jit(solution)/shard_map/pack_rows/pallas_call | solution.py:349
  3.0 8.8 %all-to-all-start = ((f32[16,7,2,128]{3,2,1,0:T(2,128)}), f32[16,7,2,128]{3,2,1,0:T(2,128)S(1)}, u32[]{:S(2)}, u32[]{:S(2)}) async-start(f32[16,7,2,128]{3,2,1,0:T(2,128)} %get-tuple-element.22), calls=%async_computation | async-start | bytes 229376 | tf_op jit(solution)/shard_map/all_to_all | solution.py:391
  11.8 0.2 collective-permute-start
  12.0 0.7 %collective-permute-start.1 = (f32[6,8,128]{2,1,0:T(8,128)S(1)}, f32[6,8,128]{2,1,0:T(8,128)S(1)}, u32[]{:S(2)}, u32[]{:S(2)}) collective-permute-start(f32[6,8,128]{2,1,0:T(8,128)S(1)} %get-tuple-element.21), channel_id=1, source_target_pairs={{1,2},{2,1},{3,4},{4,3},{5,6},{6,5},{7,8},{8,7},{9,10},{10,9},{11,... | collective-permute-start | bytes 73736 | tf_op jit(solution)/shard_map/ppermute | solution.py:396
  12.6 1.5 %sweep_planes.1 = (f32[5,16,8,128]{3,2,1,0:T(8,128)}, f32[49,8,128]{2,1,0:T(8,128)S(1)}) custom-call(f32[5,16,8,128]{3,2,1,0:T(8,128)S(1)} %get-tuple-element.13.adj_ref, f32[5,5,16,8,128]{4,3,2,1,0:T(8,128)S(1)} %get-tuple-element.14.jac_ref, f32[5,3,5,8,128]{4,3,2,1,0:T(8,128)S(1)} %get-tuple-element.15.fill_ref, ...), custom_call_target="tpu_custom_call" | custom-call | tf_op jit(solution)/shard_map/sweep_planes/pallas_call | solution.py:398
  14.2 1.6 %all-to-all-done.got_ref = f32[16,7,2,128]{3,2,1,0:T(2,128)S(1)} async-done(((f32[16,7,2,128]{3,2,1,0:T(2,128)}), f32[16,7,2,128]{3,2,1,0:T(2,128)S(1)}, u32[]{:S(2)}, u32[]{:S(2)}) %all-to-all-start) | async-done | bytes 114720 | tf_op jit(solution)/shard_map/all_to_all | solution.py:391
  15.8 2.1 %sum_rows.1.after_ref = f32[3,4096]{1,0:T(4,128)} custom-call(f32[16,7,2,128]{3,2,1,0:T(2,128)S(1)} %all-to-all-done.got_ref), custom_call_target="tpu_custom_call" | custom-call | tf_op jit(solution)/shard_map/sum_rows/pallas_call | solution.py:414
  17.9 0.0 collective-permute-done.mate_ref
  17.9 0.0 collective-permute-done.1.other_ref
  17.9 0.7 %edge_planes.1 = f32[5,16,8,128]{3,2,1,0:T(8,128)} custom-call(f32[49,8,128]{2,1,0:T(8,128)S(1)} %get-tuple-element.19.edge_ref, f32[6,8,128]{2,1,0:T(8,128)S(1)} %collective-permute-done.mate_ref, f32[6,8,128]{2,1,0:T(8,128)S(1)} %collective-permute-done.1.other_ref, f32[3,4096]{1,0:T(4,128)} %sum_rows.1.after_ref, ...), custom_call_target="tpu_custom_call", output_to_operand_aliasing={{}: (4, {})} | custom-call | tf_op jit(solution)/shard_map/edge_planes/pallas_call | solution.py:423
Async XLA Ops:
  3.0 12.8 %all-to-all-start = ((f32[16,7,2,128]{3,2,1,0:T(2,128)}), f32[16,7,2,128]{3,2,1,0:T(2,128)S(1)}, u32[]{:S(2)}, u32[]{:S(2)}) async-start(f32[16,7,2,128]{3,2,1,0:T(2,128)} %get-tuple-element.22), calls=%async_computation | async-start | bytes 229376 | tf_op jit(solution)/shard_map/all_to_all | solution.py:391
  11.8 6.1 %collective-permute-start = (f32[6,8,128]{2,1,0:T(8,128)S(1)}, f32[6,8,128]{2,1,0:T(8,128)S(1)}, u32[]{:S(2)}, u32[]{:S(2)}) collective-permute-start(f32[6,8,128]{2,1,0:T(8,128)S(1)} %get-tuple-element.20), channel_id=1, source_target_pairs={{0,1},{1,0},{2,3},{3,2},{4,5},{5,4},{6,7},{7,6},{8,9},{9,8},{10,11... | collective-permute-start | bytes 73736 | tf_op jit(solution)/shard_map/ppermute | solution.py:395
  12.0 5.9 %collective-permute-start.1 = (f32[6,8,128]{2,1,0:T(8,128)S(1)}, f32[6,8,128]{2,1,0:T(8,128)S(1)}, u32[]{:S(2)}, u32[]{:S(2)}) collective-permute-start(f32[6,8,128]{2,1,0:T(8,128)S(1)} %get-tuple-element.21), channel_id=1, source_target_pairs={{1,2},{2,1},{3,4},{4,3},{5,6},{6,5},{7,8},{8,7},{9,10},{10,9},{11,... | collective-permute-start | bytes 73736 | tf_op jit(solution)/shard_map/ppermute | solution.py:396

commit v9 on v8

--- a/solution.py
+++ b/solution.py
@@ -284,6 +284,7 @@
     inner = LAT - 1
     points = lax.broadcasted_iota(jnp.int32, (LAT, cap), 0).astype(F32)
     both = jnp.zeros((6 * LAT, LAT * LAT), F32)
+    fine = jnp.zeros((3 * LAT, LAT * LAT), F32)
     for s in range(sources):
         block = jnp.concatenate([got_ref[s, :, i, :] for i in range(cuts)], 1)
         cell = block[6:7]
@@ -303,8 +304,8 @@
         right_hi, right_lo = split_two(right)
         lhs = jnp.concatenate([left_hi, left_lo], 0)
         both = both + lax.dot_general(lhs, right_hi, NT, preferred_element_type=F32)
-        both = both + lax.dot_general(lhs, right_lo, NT, preferred_element_type=F32)
-    result = both[:3 * LAT] + both[3 * LAT:]
+        fine = fine + lax.dot_general(left_hi, right_lo, NT, preferred_element_type=F32)
+    result = both[:3 * LAT] + (both[3 * LAT:] + fine)
     for c in range(3):
         for a in range(LAT):
             out_ref[c:c + 1, a * LAT * LAT:(a + 1) * LAT * LAT] = result[c * LAT + a:c * LAT + a + 1]

time: 18.9 us -> 18.9 us (level)
  transfers between devices with their start and end apart: 3 -> 3, of which waited for: 1 -> 1; matrix products, arithmetic and copies ran while one was open for 0% -> 0% of each run, Pallas kernels for 20% -> 19%
where the time goes in v9:
time: 18.9 us; the launch traced here: 18.6 us
  starting transfers between devices  9.61 us (51%)
  Pallas kernels  6.66 us (35%)
  waiting for transfers between devices  1.65 us (9%)
  between operations  0.66 us (3%)
    all_to_all x1, starting transfers between devices, local(): lax.all_to_all(packed, 'blk', 0, 0, axis_index_groups=[spread(boxes)], ti...  8.81 us
    pallas_call x1, Pallas kernels, local(): pl.pallas_call(functools.partial(pack_kernel, boxes, cap), out_shape=(sha...  2.38 us
    pallas_call x1, Pallas kernels, local(): pl.pallas_call(sum_kernel, out_shape=shape(3, LAT ** 3), in_specs=[vmem],...  2.09 us
    all_to_all x1, waiting for transfers between devices, local(): lax.all_to_all(packed, 'blk', 0, 0, axis_index_groups=[spread(boxes)], ti...  1.64 us
    pallas_call x1, Pallas kernels, local(): pl.pallas_call(sweep_kernel, out_shape=(shape(*adjoint.shape), shape(2 *...  1.52 us
    pallas_call x1, Pallas kernels, local(): pl.pallas_call(edge_kernel, out_shape=shape(*adjoint.shape), in_specs=[vm...  0.66 us
    ppermute x1, starting transfers between devices, local(): other = lax.ppermute(to_other, 'blk', both_ways[1])  0.65 us
  transfers between devices with their start and end apart: 3, of which 1 were waited for; matrix products, arithmetic and copies ran while one was open for 0% of the time, Pallas kernels for 19%

profile of v9, /device:TPU:0, one launch (start us, length us, event | category | flops | bytes accessed | tf_op | source)
XLA Modules:
  0.0 18.6 jit_solution(4212152758809393239)
XLA Ops:
  0.6 2.4 %pack_rows.1 = (f32[16,7,2,128]{3,2,1,0:T(2,128)}, f32[6,8,128]{2,1,0:T(8,128)S(1)}, f32[6,8,128]{2,1,0:T(8,128)S(1)}, f32[5,16,8,128]{3,2,1,0:T(8,128)S(1)}, f3...) custom-call(f32[5,16,8,128]{3,2,1,0:T(8,128)} %adj_hbm.1, ...), custom_call_target="tpu_custom_call" | custom-call | tf_op jit(solution)/shard_map/pack_rows/pallas_call | solution.py:350
  3.0 8.8 %all-to-all-start = ((f32[16,7,2,128]{3,2,1,0:T(2,128)}), f32[16,7,2,128]{3,2,1,0:T(2,128)S(1)}, u32[]{:S(2)}, u32[]{:S(2)}) async-start(f32[16,7,2,128]{3,2,1,0:T(2,128)} %get-tuple-element.22), calls=%async_computation | async-start | bytes 229376 | tf_op jit(solution)/shard_map/all_to_all | solution.py:392
  11.8 0.2 collective-permute-start
  12.0 0.7 %collective-permute-start.1 = (f32[6,8,128]{2,1,0:T(8,128)S(1)}, f32[6,8,128]{2,1,0:T(8,128)S(1)}, u32[]{:S(2)}, u32[]{:S(2)}) collective-permute-start(f32[6,8,128]{2,1,0:T(8,128)S(1)} %get-tuple-element.21), channel_id=1, source_target_pairs={{1,2},{2,1},{3,4},{4,3},{5,6},{6,5},{7,8},{8,7},{9,10},{10,9},{11,... | collective-permute-start | bytes 73736 | tf_op jit(solution)/shard_map/ppermute | solution.py:397
  12.6 1.5 %sweep_planes.1 = (f32[5,16,8,128]{3,2,1,0:T(8,128)}, f32[49,8,128]{2,1,0:T(8,128)S(1)}) custom-call(f32[5,16,8,128]{3,2,1,0:T(8,128)S(1)} %get-tuple-element.13.adj_ref, f32[5,5,16,8,128]{4,3,2,1,0:T(8,128)S(1)} %get-tuple-element.14.jac_ref, f32[5,3,5,8,128]{4,3,2,1,0:T(8,128)S(1)} %get-tuple-element.15.fill_ref, ...), custom_call_target="tpu_custom_call" | custom-call | tf_op jit(solution)/shard_map/sweep_planes/pallas_call | solution.py:399
  14.2 1.6 %all-to-all-done.got_ref = f32[16,7,2,128]{3,2,1,0:T(2,128)S(1)} async-done(((f32[16,7,2,128]{3,2,1,0:T(2,128)}), f32[16,7,2,128]{3,2,1,0:T(2,128)S(1)}, u32[]{:S(2)}, u32[]{:S(2)}) %all-to-all-start) | async-done | bytes 114720 | tf_op jit(solution)/shard_map/all_to_all | solution.py:392
  15.8 2.1 %sum_rows.1.after_ref = f32[3,4096]{1,0:T(4,128)} custom-call(f32[16,7,2,128]{3,2,1,0:T(2,128)S(1)} %all-to-all-done.got_ref), custom_call_target="tpu_custom_call" | custom-call | tf_op jit(solution)/shard_map/sum_rows/pallas_call | solution.py:415
  17.9 0.0 collective-permute-done.mate_ref
  17.9 0.0 collective-permute-done.1.other_ref
  17.9 0.7 %edge_planes.1 = f32[5,16,8,128]{3,2,1,0:T(8,128)} custom-call(f32[49,8,128]{2,1,0:T(8,128)S(1)} %get-tuple-element.19.edge_ref, f32[6,8,128]{2,1,0:T(8,128)S(1)} %collective-permute-done.mate_ref, f32[6,8,128]{2,1,0:T(8,128)S(1)} %collective-permute-done.1.other_ref, f32[3,4096]{1,0:T(4,128)} %sum_rows.1.after_ref, ...), custom_call_target="tpu_custom_call", output_to_operand_aliasing={{}: (4, {})} | custom-call | tf_op jit(solution)/shard_map/edge_planes/pallas_call | solution.py:424
Async XLA Ops:
  3.0 12.8 %all-to-all-start = ((f32[16,7,2,128]{3,2,1,0:T(2,128)}), f32[16,7,2,128]{3,2,1,0:T(2,128)S(1)}, u32[]{:S(2)}, u32[]{:S(2)}) async-start(f32[16,7,2,128]{3,2,1,0:T(2,128)} %get-tuple-element.22), calls=%async_computation | async-start | bytes 229376 | tf_op jit(solution)/shard_map/all_to_all | solution.py:392
  11.8 6.1 %collective-permute-start = (f32[6,8,128]{2,1,0:T(8,128)S(1)}, f32[6,8,128]{2,1,0:T(8,128)S(1)}, u32[]{:S(2)}, u32[]{:S(2)}) collective-permute-start(f32[6,8,128]{2,1,0:T(8,128)S(1)} %get-tuple-element.20), channel_id=1, source_target_pairs={{0,1},{1,0},{2,3},{3,2},{4,5},{5,4},{6,7},{7,6},{8,9},{9,8},{10,11... | collective-permute-start | bytes 73736 | tf_op jit(solution)/shard_map/ppermute | solution.py:396
  12.0 5.9 %collective-permute-start.1 = (f32[6,8,128]{2,1,0:T(8,128)S(1)}, f32[6,8,128]{2,1,0:T(8,128)S(1)}, u32[]{:S(2)}, u32[]{:S(2)}) collective-permute-start(f32[6,8,128]{2,1,0:T(8,128)S(1)} %get-tuple-element.21), channel_id=1, source_target_pairs={{1,2},{2,1},{3,4},{4,3},{5,6},{6,5},{7,8},{8,7},{9,10},{10,9},{11,... | collective-permute-start | bytes 73736 | tf_op jit(solution)/shard_map/ppermute | solution.py:397
